TPU v7x, 32 devices: a whole 2x2x4 slice. The times are simulated.
32 devices in a mesh: dp: 8 (over y, x, core), fsdp: 4 (over z).
Axes of the slice: x: 2, y: 2, z: 4, core: 2. Of those that a mesh axis runs over, the one named last changes fastest.
Arguments:
- tokens: bfloat16 [131072, 768], P(('dp', 'fsdp')), may hold values from -6 to 6
- row_index: int32 [128, 256], P(('dp', 'fsdp')), may hold values from 0 to 1023, as said below
- row_valid: int32 [128, 256], P(('dp', 'fsdp')), may hold values from 0 to 1, as said below
- w_query: bfloat16 [768, 768], P('fsdp'), may hold values from -0.21875 to 0.21875
- w_key: bfloat16 [768, 768], P('fsdp'), may hold values from -0.21875 to 0.21875
- w_value: bfloat16 [768, 768], P('fsdp'), may hold values from -0.21875 to 0.21875
- w_out: bfloat16 [768, 768], P('fsdp'), may hold values from -0.875 to 0.875
- w_up: bfloat16 [768, 3072], P('fsdp'), may hold values from -0.21875 to 0.21875
- w_down: bfloat16 [3072, 768], P('fsdp'), may hold values from -0.109375 to 0.109375
- gain_attn: bfloat16 [768], P('fsdp'), may hold values from 0.099609375 to 1.8984375
- gain_mlp: bfloat16 [768], P('fsdp'), may hold values from 0.099609375 to 1.8984375
- w_router: bfloat16 [768], P('fsdp'), may hold values from -0.21875 to 0.21875
- cotangent: bfloat16 [131072, 768], P(('dp', 'fsdp')), may hold values from -13 to 13
Outputs:
- out_tokens: bfloat16 [131072, 768], P(('dp', 'fsdp'))
- grad_tokens: bfloat16 [131072, 768], P(('dp', 'fsdp'))
- grad_query: float32 [768, 768], P('fsdp')
- grad_key: float32 [768, 768], P('fsdp')
- grad_value: float32 [768, 768], P('fsdp')
- grad_out: float32 [768, 768], P('fsdp')
- grad_up: float32 [768, 3072], P('fsdp')
- grad_down: float32 [3072, 768], P('fsdp')
- grad_gain_attn: float32 [768], P('fsdp')
- grad_gain_mlp: float32 [768], P('fsdp')
- grad_router: float32 [768], P('fsdp')
Inputs may be any that keep to these rules, and one draw needn't show every extreme that they name: `row_index`: the 256 positions of one sequence are distinct. `row_valid`: each sequence's live slots come first; at least 42 are live, and in every draw some sequence has all 256 slots live.
All inputs are finite; a program needn't handle non-finite values.
Results may differ from a plain program's by a relative error of at most 0.012.
Values may be sent and summed in bfloat16 or wider, within the bound.
A program may use at most 256 MiB of HBM per device.

v0:
```python
import jax
import jax.numpy as jnp
from jax import lax
from jax.sharding import PartitionSpec as P

HEADS = 12
MB = 2


EPS = 1e-06
NEG = -1e30


def rms_norm(values, gain_vec):
    return values * lax.rsqrt(jnp.mean(values * values, axis=-1, keepdims=True) + EPS) * gain_vec


def gelu_tanh(values):
    return jax.nn.gelu(values, approximate=True)


def rows_by(left_mat, right_mat):
    return jnp.dot(left_mat, right_mat, preferred_element_type=jnp.float32)


def rows_by_t(left_mat, right_mat):
    return lax.dot_general(
        left_mat, right_mat, (((1,), (1,)), ((), ())), preferred_element_type=jnp.float32
    )


def outer_sum(left_mat, right_mat):
    return lax.dot_general(
        left_mat, right_mat, (((0,), (0,)), ((), ())), preferred_element_type=jnp.float32
    )


def pick_rows(tok_block, slot_index):
    return jax.vmap(lambda seq_rows, seq_index: jnp.take(seq_rows, seq_index, axis=0))(
        tok_block, slot_index
    )


def put_rows(tok_block, slot_index, addend):
    return jax.vmap(lambda seq_rows, seq_index, seq_add: seq_rows.at[seq_index].add(seq_add))(
        tok_block, slot_index, addend
    )


def attention_scores(queries, keys_head, pair_mask, score_scale):
    raw_scores = (
        jnp.einsum("sqhe,skhe->shqk", queries, keys_head, preferred_element_type=jnp.float32)
        * score_scale
    )
    return jnp.where(pair_mask[:, None], raw_scores, NEG)


def forward_block(picked, live_slots, slot_index, gathered, head_count):
    w_query, w_key, w_value, w_out, w_up, w_down, gain_attn, gain_mlp, w_router = gathered
    seq_count, slots, model_width = picked.shape
    head_size = model_width // head_count
    score_scale = head_size ** (-0.5)
    flat_rows = picked.reshape(seq_count * slots, model_width)
    rows_wide = flat_rows.astype(jnp.float32)
    router_gate = jax.nn.sigmoid(rows_by(flat_rows, w_router))
    normed_attn = rms_norm(rows_wide, gain_attn.astype(jnp.float32)).astype(jnp.bfloat16)
    head_shape = (seq_count, slots, head_count, head_size)
    queries = rows_by(normed_attn, w_query).astype(jnp.bfloat16).reshape(head_shape)
    keys_head = rows_by(normed_attn, w_key).astype(jnp.bfloat16).reshape(head_shape)
    values_head = rows_by(normed_attn, w_value).astype(jnp.bfloat16).reshape(head_shape)
    pair_mask = (slot_index[:, None, :] < slot_index[:, :, None]) & (live_slots[:, None, :] > 0) | (
        slot_index[:, None, :] == slot_index[:, :, None]
    )
    scores = attention_scores(queries, keys_head, pair_mask, score_scale)
    row_top = jnp.max(scores, axis=-1, keepdims=True)
    row_total = jnp.sum(jnp.exp(scores - row_top), axis=-1, keepdims=True)
    log_total = row_top + jnp.log(row_total)
    probs = jnp.exp(scores - log_total).astype(jnp.bfloat16)
    mixed_raw = jnp.einsum(
        "shqk,skhe->sqhe", probs, values_head, preferred_element_type=jnp.float32
    )
    mixed_heads = mixed_raw.astype(jnp.bfloat16).reshape(seq_count * slots, model_width)
    attn_out = rows_by(mixed_heads, w_out)
    hidden = rows_wide + router_gate[:, None] * attn_out
    normed_mlp = rms_norm(hidden, gain_mlp.astype(jnp.float32)).astype(jnp.bfloat16)
    upward = rows_by(normed_mlp, w_up)
    active = gelu_tanh(upward).astype(jnp.bfloat16)
    down_out = rows_by(active, w_down)
    live_col = live_slots.reshape(-1).astype(jnp.float32)[:, None]
    change = (router_gate[:, None] * attn_out + down_out) * live_col
    saved_state = (
        rows_wide,
        router_gate,
        normed_attn,
        queries,
        keys_head,
        values_head,
        pair_mask,
        log_total,
        mixed_heads,
        attn_out,
        hidden,
        normed_mlp,
        upward,
        active,
    )
    return (change, saved_state)


def backward_block(upstream, live_slots, saved_state, gathered, head_count):
    (
        rows_wide,
        router_gate,
        normed_attn,
        queries,
        keys_head,
        values_head,
        pair_mask,
        log_total,
        mixed_heads,
        attn_out,
        hidden,
        normed_mlp,
        upward,
        active,
    ) = saved_state
    w_query, w_key, w_value, w_out, w_up, w_down, gain_attn, gain_mlp, w_router = gathered
    seq_count, slots, _, head_size = queries.shape
    model_width = head_count * head_size
    total_rows = seq_count * slots
    score_scale = head_size ** (-0.5)
    live_col = live_slots.reshape(-1).astype(jnp.float32)[:, None]
    d_change = upstream * live_col
    d_down = d_change.astype(jnp.bfloat16)
    g_down = outer_sum(active, d_down)
    d_active = rows_by_t(d_down, w_down)
    _, gelu_pull = jax.vjp(gelu_tanh, upward)
    d_up = gelu_pull(d_active)[0].astype(jnp.bfloat16)
    g_up = outer_sum(normed_mlp, d_up)
    d_normed_mlp = rows_by_t(d_up, w_up)
    _, second_pull = jax.vjp(rms_norm, hidden, gain_mlp.astype(jnp.float32))
    d_hidden, g_gain_mlp = second_pull(d_normed_mlp)
    d_branch = d_change + d_hidden
    d_gate = jnp.sum(d_branch * attn_out, axis=-1)
    d_logit = d_gate * router_gate * (1.0 - router_gate)
    g_router = jnp.dot(d_logit, rows_wide, precision=lax.Precision.HIGHEST)
    d_attn = (d_branch * router_gate[:, None]).astype(jnp.bfloat16)
    g_out = outer_sum(mixed_heads, d_attn)
    d_mixed = (
        rows_by_t(d_attn, w_out)
        .astype(jnp.bfloat16)
        .reshape(seq_count, slots, head_count, head_size)
    )
    scores = attention_scores(queries, keys_head, pair_mask, score_scale)
    soft_wide = jnp.exp(scores - log_total)
    d_values = jnp.einsum(
        "shqk,sqhe->skhe",
        soft_wide.astype(jnp.bfloat16),
        d_mixed,
        preferred_element_type=jnp.float32,
    )
    d_probs = jnp.einsum(
        "sqhe,skhe->shqk", d_mixed, values_head, preferred_element_type=jnp.float32
    )
    d_scores = (
        soft_wide * (d_probs - jnp.sum(soft_wide * d_probs, axis=-1, keepdims=True))
    ).astype(jnp.bfloat16)
    d_queries = (
        jnp.einsum("shqk,skhe->sqhe", d_scores, keys_head, preferred_element_type=jnp.float32)
        * score_scale
    )
    d_keys = (
        jnp.einsum("shqk,sqhe->skhe", d_scores, queries, preferred_element_type=jnp.float32)
        * score_scale
    )
    d_queries = d_queries.astype(jnp.bfloat16).reshape(total_rows, model_width)
    d_keys = d_keys.astype(jnp.bfloat16).reshape(total_rows, model_width)
    d_values = d_values.astype(jnp.bfloat16).reshape(total_rows, model_width)
    g_query = outer_sum(normed_attn, d_queries)
    g_key = outer_sum(normed_attn, d_keys)
    g_value = outer_sum(normed_attn, d_values)
    d_normed = (
        rows_by_t(d_queries, w_query) + rows_by_t(d_keys, w_key) + rows_by_t(d_values, w_value)
    )
    _, first_pull = jax.vjp(rms_norm, rows_wide, gain_attn.astype(jnp.float32))
    d_first, g_gain_attn = first_pull(d_normed)
    d_picked = d_first + d_hidden + d_logit[:, None] * w_router.astype(jnp.float32)[None, :]
    grads = (g_query, g_key, g_value, g_out, g_up, g_down, g_gain_attn, g_gain_mlp, g_router)
    return (d_picked, grads)


def body(
    tokens,
    row_index,
    row_valid,
    w_query,
    w_key,
    w_value,
    w_out,
    w_up,
    w_down,
    gain_attn,
    gain_mlp,
    w_router,
    cotangent,
):
    shards = (w_query, w_key, w_value, w_out, w_up, w_down, gain_attn, gain_mlp, w_router)
    head_count = HEADS
    seqs_dev = row_index.shape[0]
    slots = row_index.shape[1]
    model_width = tokens.shape[1]
    seq_len = tokens.shape[0] // seqs_dev
    micro_count = MB
    per_micro = seqs_dev // micro_count
    tok_blocks = tokens.reshape(micro_count, per_micro, seq_len, model_width)
    upstream_blocks = cotangent.reshape(micro_count, per_micro, seq_len, model_width)
    index_blocks = row_index.reshape(micro_count, per_micro, slots)
    live_blocks = row_valid.reshape(micro_count, per_micro, slots)
    outputs = []
    input_grads = []
    summed = None
    for micro in range(micro_count):
        gathered = (
            lax.all_gather(shards[0], "fsdp", axis=0, tiled=True),
            lax.all_gather(shards[1], "fsdp", axis=0, tiled=True),
            lax.all_gather(shards[2], "fsdp", axis=0, tiled=True),
            lax.all_gather(shards[3], "fsdp", axis=0, tiled=True),
            lax.all_gather(shards[4], "fsdp", axis=0, tiled=True),
            lax.all_gather(shards[5], "fsdp", axis=0, tiled=True),
            lax.all_gather(shards[6], "fsdp", axis=0, tiled=True),
            lax.all_gather(shards[7], "fsdp", axis=0, tiled=True),
            lax.all_gather(shards[8], "fsdp", axis=0, tiled=True),
        )
        tok_block = tok_blocks[micro]
        slot_index = index_blocks[micro]
        live_slots = live_blocks[micro]
        picked = pick_rows(tok_block, slot_index)
        change, saved_state = forward_block(picked, live_slots, slot_index, gathered, head_count)
        outputs.append(
            put_rows(
                tok_block.astype(jnp.float32),
                slot_index,
                change.reshape(per_micro, slots, model_width),
            ).astype(jnp.bfloat16)
        )
        gathered_back = (
            lax.all_gather(shards[0], "fsdp", axis=0, tiled=True),
            lax.all_gather(shards[1], "fsdp", axis=0, tiled=True),
            lax.all_gather(shards[2], "fsdp", axis=0, tiled=True),
            lax.all_gather(shards[3], "fsdp", axis=0, tiled=True),
            lax.all_gather(shards[4], "fsdp", axis=0, tiled=True),
            lax.all_gather(shards[5], "fsdp", axis=0, tiled=True),
            lax.all_gather(shards[6], "fsdp", axis=0, tiled=True),
            lax.all_gather(shards[7], "fsdp", axis=0, tiled=True),
            lax.all_gather(shards[8], "fsdp", axis=0, tiled=True),
        )
        upstream_block = upstream_blocks[micro]
        upstream = (
            pick_rows(upstream_block, slot_index)
            .astype(jnp.float32)
            .reshape(per_micro * slots, model_width)
        )
        d_picked, grads = backward_block(
            upstream, live_slots, saved_state, gathered_back, head_count
        )
        input_grads.append(
            put_rows(
                upstream_block.astype(jnp.float32),
                slot_index,
                d_picked.reshape(per_micro, slots, model_width),
            ).astype(jnp.bfloat16)
        )
        summed = grads if summed is None else jax.tree.map(jnp.add, summed, grads)
    summed = lax.psum_scatter(summed, "fsdp", scatter_dimension=0, tiled=True)
    summed = lax.psum(summed, "dp")
    out_tokens = jnp.stack(outputs).reshape(tokens.shape)
    grad_tokens = jnp.stack(input_grads).reshape(tokens.shape)
    return (
        out_tokens,
        grad_tokens,
        summed[0],
        summed[1],
        summed[2],
        summed[3],
        summed[4],
        summed[5],
        summed[6],
        summed[7],
        summed[8],
    )


def solution(mesh):
    placed = (
        P(("dp", "fsdp"), None),
        P(("dp", "fsdp"), None),
        P(("dp", "fsdp"), None),
        P("fsdp", None),
        P("fsdp", None),
        P("fsdp", None),
        P("fsdp", None),
        P("fsdp", None),
        P("fsdp", None),
        P("fsdp"),
        P("fsdp"),
        P("fsdp"),
        P(("dp", "fsdp"), None),
    )
    return jax.shard_map(
        body,
        mesh=mesh,
        in_specs=placed,
        out_specs=(
            P(("dp", "fsdp"), None),
            P(("dp", "fsdp"), None),
            P("fsdp", None),
            P("fsdp", None),
            P("fsdp", None),
            P("fsdp", None),
            P("fsdp", None),
            P("fsdp", None),
            P("fsdp"),
            P("fsdp"),
            P("fsdp"),
        ),
        check_vma=False,
    )
```

profile of v0, /device:TPU:0, one launch (start us, length us, event | category | flops | bytes accessed | tf_op | source)
XLA Modules:
  0.0 1288.7 jit_solution(14897447610817180197)
XLA Ops:
  11.8 5.0 fusion.102
  17.2 3.3 fusion.101
  20.6 7.2 gather_fusion.1
  27.8 7.4 gather_fusion
  39.2 13.7 %all-reduce.9 = (bf16[768]{0:T(1024)(128)(2,1)S(1)}, bf16[768]{0:T(1024)(128)(2,1)S(1)}, bf16[768]{0:T(1024)(128)(2,1)S(1)}) all-reduce(bf16[768]{0:T(1024)(128)(2,1)S(1)} %dynamic-update-slice.1, bf16[768]{0:T(1024)(128)(2,1)S(1)} %dynamic-update-slice, bf16[768]{0:T(1024)(128)(2,1)S(1)} %dynamic-update-slice.2), channel_id=1, replica_groups=mesh['dp'=8,'fsdp'=4] {'fsdp'}, use_global_device_ids=true, to_apply=%add.1 | all-reduce | flops 2304 | bytes 9216
  52.9 10.1 gather_fusion.2
  63.0 7.2 gather_fusion.3
  78.8 3.2 convolution_convert_fusion.10
  83.7 2.5 convolution_convert_fusion.9
  89.7 15.4 %all-gather.7.cloned.1.call-done = bf16[768,768]{1,0:T(8,128)(2,1)} async-done(((bf16[192,768]{1,0:T(8,128)(2,1)}), bf16[768,768]{1,0:T(8,128)(2,1)}) %all-gather.7.cloned.1.call-update) | async-done | bytes 1179664 | tf_op jit(solution)/shard_map/all_gather | solution.py:226
  105.1 3.2 convolution_convert_fusion.11
  108.3 2.3 copy.88
  110.6 3.3 reshape.345
  121.2 14.9 %all-gather.13.cloned.1.call-done = bf16[768,768]{1,0:T(8,128)(2,1)} async-done(((bf16[192,768]{1,0:T(8,128)(2,1)}), bf16[768,768]{1,0:T(8,128)(2,1)}) %all-gather.13.cloned.1.call-update) | async-done | bytes 1179664 | tf_op jit(solution)/shard_map/all_gather | solution.py:227
  136.1 3.6 multiply_reduce_fusion.9
  139.7 86.4 %all-gather.17.cloned.1.call-done = bf16[3072,768]{1,0:T(8,128)(2,1)} async-done(((bf16[768,768]{1,0:T(8,128)(2,1)}), bf16[3072,768]{1,0:T(8,128)(2,1)}) %all-gather.17.cloned.1.call-update) | async-done | bytes 4718608 | tf_op jit(solution)/shard_map/all_gather | solution.py:229
  226.1 8.1 fusion.107
  234.1 81.3 %all-gather.15.cloned.1.call-done = bf16[768,3072]{1,0:T(8,128)(2,1)} async-done(((bf16[192,3072]{1,0:T(8,128)(2,1)}), bf16[768,3072]{1,0:T(8,128)(2,1)}) %all-gather.15.cloned.1.call-update) | async-done | bytes 4718608 | tf_op jit(solution)/shard_map/all_gather | solution.py:228
  315.4 12.3 fusion.6
  327.7 3.3 multiply_reduce_fusion.3
  336.5 3.2 reshape.359
  339.7 5.5 multiply_reduce_fusion.1
  347.2 2.3 fusion.43
  359.4 2.8 fusion.25
  367.3 2.3 convolution_convert_fusion.5
  373.0 2.7 fusion.15
  380.3 2.3 copy.96
  382.6 2.6 reshape.351
  386.1 4.3 fusion.47
  392.7 5.9 fusion.110
  398.7 8.8 fusion.13
  407.5 2.8 multiply_reduce_fusion.2
  413.7 2.2 convolution_add_fusion.2
  417.5 2.4 convolution_convert_fusion.1
  420.4 4.5 fusion.49
  429.6 4.2 multiply_reduce_fusion
  433.8 4.7 multiply_convert_fusion
  447.9 2.2 convolution_add_fusion.5
  450.5 4.8 fusion.97
  455.4 5.6 convolution_add_fusion.1
  462.1 5.5 fusion.100
  467.6 5.7 convolution_add_fusion
  475.2 3.1 convert_element_type.250
  478.3 3.1 convert_element_type.264
  481.5 3.2 convert_element_type.218
  484.6 3.2 convert_element_type.235
  489.1 2.2 fusion.112
  498.2 7.7 add_multiply_fusion.1
  505.9 6.6 reduce-scatter.11.cloned.1.call-done
  512.5 50.4 %reduce-scatter.9.cloned.1.call-done = f32[192,768]{1,0:T(8,128)} async-done(((f32[768,768]{1,0:T(8,128)}), f32[192,768]{1,0:T(8,128)}) %reduce-scatter.9.cloned.1.call-update) | async-done | bytes 589840 | tf_op jit(solution)/shard_map/reduce_scatter | solution.py:274
  563.0 50.3 %reduce-scatter.7.cloned.1.call-done = f32[192,768]{1,0:T(8,128)} async-done(((f32[768,768]{1,0:T(8,128)}), f32[192,768]{1,0:T(8,128)}) %reduce-scatter.7.cloned.1.call-update) | async-done | bytes 589840 | tf_op jit(solution)/shard_map/reduce_scatter | solution.py:274
  613.3 163.2 %reduce-scatter.15.cloned.1.call-done = f32[192,3072]{1,0:T(8,128)} async-done(((f32[768,3072]{1,0:T(8,128)}), f32[192,3072]{1,0:T(8,128)}) %reduce-scatter.15.cloned.1.call-update) | async-done | bytes 2359312 | tf_op jit(solution)/shard_map/reduce_scatter | solution.py:274
  776.4 164.4 %reduce-scatter.17.cloned.1.call-done = f32[768,768]{1,0:T(8,128)} async-done(((f32[3072,768]{1,0:T(8,128)}), f32[768,768]{1,0:T(8,128)}) %reduce-scatter.17.cloned.1.call-update) | async-done | bytes 2359312 | tf_op jit(solution)/shard_map/reduce_scatter | solution.py:274
  941.5 18.6 %all-reduce.8 = (f32[768]{0:T(1024)S(1)}, f32[768]{0:T(1024)S(1)}, f32[768]{0:T(1024)S(1)}) all-reduce(f32[768]{0:T(1024)S(1)} %add.255, f32[768]{0:T(1024)S(1)} %add.256, f32[768]{0:T(1024)S(1)} %add.257), channel_id=8, replica_groups=mesh['dp'=8,'fsdp'=4] {'fsdp'}, use_global_device_ids=true, to_apply=%region_34.36.clone | all-reduce | flops 2304 | bytes 18432
  960.3 71.1 %scatter_fusion.2 = f32[2,1024,768]{2,1,0:T(8,128)} fusion(f32[2,1024,768]{2,1,0:T(8,128)} %convert_element_type.250, s32[512]{0:T(512)S(1)} %bitcast.238, f32[512,768]{1,0:T(8,128)} %get-tuple-element.51), kind=kCustom, calls=%fused_computation.6 | custom fusion | flops 393216 | bytes 4722688 | tf_op jit(solution)/shard_map/vmap()/scatter-add | solution.py:45
  1031.4 69.0 %scatter_fusion = f32[2,1024,768]{2,1,0:T(8,128)} fusion(f32[2,1024,768]{2,1,0:T(8,128)} %convert_element_type.218, s32[512]{0:T(512)S(1)} %bitcast.239, f32[512,768]{1,0:T(8,128)S(1)} %copy-done.76), kind=kCustom, calls=%fused_computation.4 | custom fusion | flops 393216 | bytes 4722688 | tf_op jit(solution)/shard_map/vmap()/scatter-add | solution.py:45
  1100.4 68.8 %scatter_fusion.3 = f32[2,1024,768]{2,1,0:T(8,128)} fusion(f32[2,1024,768]{2,1,0:T(8,128)} %convert_element_type.264, s32[512]{0:T(512)S(1)} %bitcast.236, f32[512,768]{1,0:T(8,128)S(1)} %get-tuple-element.52), kind=kCustom, calls=%fused_computation.7 | custom fusion | flops 393216 | bytes 4722688 | tf_op jit(solution)/shard_map/vmap()/scatter-add | solution.py:45
  1169.1 7.3 add_multiply_fusion
  1176.4 68.5 %scatter_fusion.1 = f32[2,1024,768]{2,1,0:T(8,128)} fusion(f32[2,1024,768]{2,1,0:T(8,128)} %convert_element_type.235, s32[512]{0:T(512)S(1)} %bitcast.237, f32[512,768]{1,0:T(8,128)S(1)} %add_multiply_fusion), kind=kCustom, calls=%fused_computation.5 | custom fusion | flops 393216 | bytes 4722688 | tf_op jit(solution)/shard_map/vmap()/scatter-add | solution.py:45
  1244.9 12.3 all-reduce.6
  1257.3 3.2 convert_bitcast_fusion.1
  1262.2 3.7 pad_maximum_fusion.1
  1265.9 2.3 slice-done.3
  1269.2 3.2 pad_maximum_fusion
  (395 shorter events, 104.6 us)
Async XLA Ops:
  7.2 4.0 copy-start.82
  7.2 71.6 %all-gather.9.cloned.1.call-start = ((), (), s32[]{:S(2)}) async-start(), calls=%async_computation.7 | async-start | bytes 1474560 | tf_op jit(solution)/shard_map/all_gather | solution.py:224
  7.9 75.8 %all-gather.11.cloned.1.call-start = ((), (), s32[]{:S(2)}) async-start(), calls=%async_computation.8 | async-start | bytes 1474560 | tf_op jit(solution)/shard_map/all_gather | solution.py:225
  8.7 96.4 %all-gather.7.cloned.1.call-start = ((), (), s32[]{:S(2)}) async-start(), calls=%async_computation.6 | async-start | bytes 1474560 | tf_op jit(solution)/shard_map/all_gather | solution.py:226
  9.4 126.7 %all-gather.13.cloned.1.call-start = ((), (), s32[]{:S(2)}) async-start(), calls=%async_computation.9 | async-start | bytes 1474560 | tf_op jit(solution)/shard_map/all_gather | solution.py:227
  10.0 216.1 %all-gather.17.cloned.1.call-start = ((), (), s32[]{:S(2)}) async-start(), calls=%async_computation.11 | async-start | bytes 5898240 | tf_op jit(solution)/shard_map/all_gather | solution.py:229
  10.6 304.8 %all-gather.15.cloned.1.call-start = ((), (), s32[]{:S(2)}) async-start(), calls=%async_computation.10 | async-start | bytes 5898240 | tf_op jit(solution)/shard_map/all_gather | solution.py:228
  11.1 494.8 %reduce-scatter.13.cloned.1.call-start = ((), (), s32[]{:S(2)}) async-start(), calls=%async_computation.15 | async-start | bytes 2949120 | tf_op jit(solution)/shard_map/reduce_scatter | solution.py:274
  11.8 5.0 slice-start.8
  11.8 5.4 slice-start.9
  16.8 3.7 copy-start.3
  27.8 7.5 copy-start.64
  35.2 3.5 copy-start.103
  35.2 3.7 copy-start.104
  37.2 25.9 %copy-start.87 = (f32[1,2,2,128]{3,1,2,0:T(2,128)}, f32[1,2,2,128]{3,1,2,0:T(2,128)S(1)}, u32[]{:S(2)}) copy-start(f32[1,2,2,128]{3,1,2,0:T(2,128)S(1)} %copy.138) | copy-start | bytes 6148
  52.9 10.2 copy-start.92
  52.9 10.1 copy-start.6
  63.0 7.3 copy-start.91
  73.8 4.7 copy-start.85
  74.4 4.2 copy-start.9
  78.8 3.2 copy-start.78
  83.7 30.2 %copy-start.57 = (bf16[2,256,12,64]{1,0,3,2:T(2,128)(2,1)}, bf16[2,256,12,64]{1,0,3,2:T(2,128)(2,1)S(1)}, u32[]{:S(2)}) copy-start(bf16[2,256,12,64]{1,0,3,2:T(2,128)(2,1)S(1)} %reshape.346) | copy-start | bytes 2359300
  89.6 24.2 %copy-start.58 = (bf16[2,256,12,64]{1,0,3,2:T(2,128)(2,1)}, bf16[2,256,12,64]{1,0,3,2:T(2,128)(2,1)S(1)}, u32[]{:S(2)}) copy-start(bf16[2,256,12,64]{1,0,3,2:T(2,128)(2,1)S(1)} %reshape.347) | copy-start | bytes 2359300
  139.7 191.4 %copy-start.19 = (f32[512,768]{1,0:T(8,128)}, f32[512,768]{1,0:T(8,128)S(1)}, u32[]{:S(2)}) copy-start(f32[512,768]{1,0:T(8,128)S(1)} %get-tuple-element.40) | copy-start | bytes 4718596
  315.4 12.3 copy-start.98
  327.7 3.4 copy-start.65
  327.7 3.4 copy-start.27
  327.7 3.4 copy-start.38
  336.5 8.8 slice-start.4
  339.7 5.6 slice-start.5
  391.7 7.0 slice-start.12
  392.7 17.7 %copy-start.13 = (f32[512,768]{1,0:T(8,128)}, f32[512,768]{1,0:T(8,128)S(1)}, u32[]{:S(2)}) copy-start(f32[512,768]{1,0:T(8,128)S(1)} %get-tuple-element.44) | copy-start | bytes 4718596
  392.7 17.7 %copy-start.40 = (f32[512,768]{1,0:T(8,128)}, f32[512,768]{1,0:T(8,128)S(1)}, u32[]{:S(2)}) copy-start(f32[512,768]{1,0:T(8,128)S(1)} %get-tuple-element.85) | copy-start | bytes 4718596
  392.7 5.9 slice-start.13
  416.0 96.5 %reduce-scatter.11.cloned.1.call-start = ((), (), s32[]{:S(2)}) async-start(), calls=%async_computation.14 | async-start | bytes 2949120 | tf_op jit(solution)/shard_map/reduce_scatter | solution.py:274
  417.5 9.6 copy-start.21
  429.3 133.7 %reduce-scatter.9.cloned.1.call-start = ((), (), s32[]{:S(2)}) async-start(), calls=%async_computation.13 | async-start | bytes 2949120 | tf_op jit(solution)/shard_map/reduce_scatter | solution.py:274
  433.8 4.7 copy-start.50
  444.0 169.3 %reduce-scatter.7.cloned.1.call-start = ((), (), s32[]{:S(2)}) async-start(), calls=%async_computation.12 | async-start | bytes 2949120 | tf_op jit(solution)/shard_map/reduce_scatter | solution.py:274
  450.2 5.2 copy-start.14
  450.2 326.3 %reduce-scatter.15.cloned.1.call-start = ((), (), s32[]{:S(2)}) async-start(), calls=%async_computation.16 | async-start | bytes 11796480 | tf_op jit(solution)/shard_map/reduce_scatter | solution.py:274
  450.5 4.9 copy-start.48
  460.9 6.6 slice-start.6
  460.9 479.9 %reduce-scatter.17.cloned.1.call-start = ((), (), s32[]{:S(2)}) async-start(), calls=%async_computation.17 | async-start | bytes 11796480 | tf_op jit(solution)/shard_map/reduce_scatter | solution.py:274
  462.0 5.5 slice-start.7
  462.0 5.5 copy-start.73
  473.3 799.2 %all-reduce.12.cloned.1.call-start = ((), (), s32[]{:S(2)}) async-start(), calls=%async_computation.18 | async-start | bytes 14155776 | tf_op jit(solution)/shard_map/psum | solution.py:275
  484.6 3.2 copy-start.94
  484.6 4.0 copy-start.86
  484.6 4.0 copy-start.12
  484.6 4.4 copy-start.84
  484.6 4.5 copy-start.52
  487.8 3.5 copy-start.54
  492.3 4.8 slice-start.10
  494.9 3.3 slice-start.11
  960.3 71.1 %copy-start.76 = (f32[512,768]{1,0:T(8,128)S(1)}, f32[512,768]{1,0:T(8,128)}, u32[]{:S(2)}) copy-start(f32[512,768]{1,0:T(8,128)} %add_multiply_fusion.1) | copy-start | bytes 4718596
  1100.4 68.8 %copy-start.41 = (f32[512,768]{1,0:T(8,128)S(1)}, f32[512,768]{1,0:T(8,128)}, u32[]{:S(2)}) copy-start(f32[512,768]{1,0:T(8,128)} %copy-done.40) | copy-start | bytes 4718596
  1257.3 4.6 copy-start
  1261.9 4.1 slice-start.2
  1261.9 6.7 slice-start
  1262.2 6.1 slice-start.3
  1262.2 6.7 slice-start.1
  1272.4 5.9 copy-start.81
  1272.4 6.7 copy-start.75
  (68 other events, 131.9 us)
Sparse Core Ops, SparseCore 0:
  9.6 33.1 all-gather.8
  44.3 29.5 all-gather.10
  75.5 29.5 all-gather.6
  106.5 29.5 all-gather.12
  137.5 88.5 all-gather.16
  227.5 87.8 all-gather.14
  416.1 46.4 reduce-scatter.12
  465.0 47.5 reduce-scatter.10
  515.4 47.5 reduce-scatter.8
  565.7 47.5 reduce-scatter.6
  615.6 160.7 reduce-scatter.14
  778.7 162.1 reduce-scatter.16
  944.9 114.7 all-reduce.11
where the time goes:
time: 1300 us; the launch traced here: 1290 us
  waiting for transfers between devices  637 us (49%)
  other arithmetic  324 us (25%)
  matrix products  158 us (12%)
  local copies, waits for them, and re-layouts  107 us (8%)
  blocking collectives  44.6 us (3%)
  between operations  17.3 us (1%)
    reduce_scatter x6, waiting for transfers between devices, body(): summed = lax.psum_scatter(summed, 'fsdp', scatter_dimension=0, tiled=True)  435 us
    scatter-add x4, other arithmetic, put_rows(): seq_rows.at[seq_index].add(seq_add)  277 us
    all_gather x1, waiting for transfers between devices, body(): lax.all_gather(shards[5], 'fsdp', axis=0, tiled=True)  86.4 us
    all_gather x1, waiting for transfers between devices, body(): lax.all_gather(shards[4], 'fsdp', axis=0, tiled=True)  81.3 us
    dot_general x14, matrix products, rows_by(): return jnp.dot(left_mat, right_mat, preferred_element_type=jnp.float32)  58.1 us
    dot_general x12, matrix products, outer_sum(): lax.dot_general(left_mat, right_mat, (((0,), (0,)), ((), ())), preferred_...  35.1 us
    unnamed x271, local copies, waits for them, and re-layouts  33.8 us
    unnamed x2, blocking collectives  32.2 us
  transfers between devices with their start and end apart: 13, of which 9 were waited for; matrix products, arithmetic and copies ran while one was open for 36% of the time, Pallas kernels for 0%

commit v1 on v0

v1 whole, which is shorter than its diff:
```python
import functools

import jax
import jax.numpy as jnp
from jax import lax
from jax.experimental import pallas as pl
from jax.experimental.pallas import tpu as pltpu

from jax.sharding import PartitionSpec as P

HEADS = 12
EPS = 1e-06
NEG = -1e30
BF = jnp.bfloat16
F32 = jnp.float32
GATE, R1, R2, LIVE, DLOG, POS = range(6)


def nn(a, b):
    return lax.dot_general(a, b, (((1,), (0,)), ((), ())), preferred_element_type=F32)


def nt(a, b):
    return lax.dot_general(a, b, (((1,), (1,)), ((), ())), preferred_element_type=F32)


def tn(a, b):
    return lax.dot_general(a, b, (((0,), (0,)), ((), ())), preferred_element_type=F32)


def flat(v):
    return v.reshape(-1, v.shape[-1])


def pick_phase(tokens, cot, idx, valid, picked, up, cols, tok_buf, tok_sem):
    seqs, slots = idx.shape
    length = tokens.shape[0] // seqs

    def fetch(t, slot):
        src = tokens if t % 2 == 0 else cot
        return pltpu.make_async_copy(
            src.at[pl.ds((t // 2) * length, length)], tok_buf[slot], tok_sem.at[slot]
        )

    fetch(0, 0).start()
    fetch(1, 1).start()
    pad = jnp.zeros((8 - seqs, slots), F32) if seqs < 8 else None
    for what, k in ((idx, POS), (valid, LIVE)):
        rows8 = what[...].astype(F32)
        if pad is not None:
            rows8 = jnp.concatenate([rows8, pad], axis=0)
        turned = rows8.T
        for s in range(seqs):
            cols[s * slots : (s + 1) * slots, k : k + 1] = turned[:, s : s + 1]
    lane = lax.broadcasted_iota(jnp.int32, (slots, length), 1).astype(F32)
    for s in range(seqs):
        rows = slice(s * slots, (s + 1) * slots)
        hot = jnp.where(lane == cols[rows, POS : POS + 1], 1.0, 0.0).astype(BF)
        for b, dst in ((0, picked), (1, up)):
            fetch(2 * s + b, b).wait()
            dst[rows, :] = nn(hot, tok_buf[b][...]).astype(BF)
            if s + 1 < seqs:
                fetch(2 * s + 2 + b, b).start()


def norm_phase(picked, gains, cols, na, tile=256):
    total = picked.shape[0]

    @pl.loop(0, total // tile)
    def _(i):
        rows = pl.ds(pl.multiple_of(i * tile, tile), tile)
        x = picked[rows, :].astype(F32)
        cols[rows, GATE : GATE + 1] = jax.nn.sigmoid(
            jnp.sum(x * gains[2:3, :], axis=1, keepdims=True)
        )
        r1 = lax.rsqrt(jnp.mean(x * x, axis=1, keepdims=True) + EPS)
        cols[rows, R1 : R1 + 1] = r1
        na[rows, :] = (x * r1 * gains[0:1, :]).astype(BF)


def qkv_phase(na, wa, qkv, scale):
    width = na.shape[1]
    for m in range(3):

        @pl.loop(0, width // 256)
        def _(n):
            at = pl.ds(pl.multiple_of(n * 256, 256), 256)
            out = nn(na[...], flat(wa[m, :, :, :, :, at]))
            if m == 0:
                out = out * scale
            qkv[m, :, at] = out.astype(BF)


def two_heads(v2, low_half):
    zero = jnp.zeros_like(v2)
    return jnp.concatenate([jnp.where(low_half, v2, zero), jnp.where(low_half, zero, v2)], axis=0)


def attention_forward(idx, valid, cols, qkv, probs, mixed, s):
    slots = idx.shape[1]
    width = mixed.shape[1]
    rows = pl.ds(pl.multiple_of(s * slots, slots), slots)
    low_half = lax.broadcasted_iota(jnp.int32, (slots, 128), 1) < 64
    mine = cols[rows, POS : POS + 1]
    other = idx[pl.ds(s, 1), :].astype(F32)
    seen = ((other < mine) & (valid[pl.ds(s, 1), :] > 0)) | (other == mine)
    bias = jnp.where(seen, 0.0, NEG)
    bias = jnp.concatenate([bias, bias], axis=0)
    for p in range(width // 128):
        at = slice(p * 128, p * 128 + 128)
        q2 = two_heads(qkv[0, rows, at], low_half)
        scores = nt(q2, qkv[1, rows, at]) + bias
        e = jnp.exp(scores - jnp.max(scores, axis=1, keepdims=True))
        pr = (e * (1.0 / jnp.sum(e, axis=1, keepdims=True))).astype(BF)
        probs[s * (width // 128) + p] = pr
        o = nn(pr, qkv[2, rows, at])
        mixed[rows, at] = jnp.where(low_half, o[:slots], o[slots:]).astype(BF)


def attention_backward(qkv, probs, mixed, dmix, s, slots, scale):
    width = mixed.shape[1]
    rows = pl.ds(pl.multiple_of(s * slots, slots), slots)
    low_half = lax.broadcasted_iota(jnp.int32, (slots, 128), 1) < 64
    for p in range(width // 128):
        at = slice(p * 128, p * 128 + 128)
        do2 = two_heads(dmix[rows, at], low_half)
        o2 = mixed[rows, at].astype(F32)
        o2 = jnp.concatenate([o2, o2], axis=0)
        delta = jnp.sum(do2.astype(F32) * o2, axis=1, keepdims=True)
        k2 = qkv[1, rows, at]
        dp = nt(do2, qkv[2, rows, at])
        pr = probs[s * (width // 128) + p]
        ds = (pr.astype(F32) * (dp - delta)).astype(BF)
        q2 = two_heads(qkv[0, rows, at], low_half)
        dq = nn(ds, k2) * scale
        qkv[0, rows, at] = jnp.where(low_half, dq[:slots], dq[slots:]).astype(BF)
        qkv[1, rows, at] = tn(ds, q2).astype(BF)
        qkv[2, rows, at] = tn(pr, do2).astype(BF)


def out_phase(mixed, wa, attn_out):
    width = mixed.shape[1]

    @pl.loop(0, width // 256)
    def _(n):
        at = pl.ds(pl.multiple_of(n * 256, 256), 256)
        attn_out[:, at] = nn(mixed[...], flat(wa[3, :, :, :, :, at]))


def mid_norm(picked, attn_out, up, gains, cols, nm, nmt, dd, down, dnm, tile=256):
    total = picked.shape[0]
    for i in range(total // tile):
        rows = slice(i * tile, (i + 1) * tile)
        hidden = picked[rows, :].astype(F32) + cols[rows, GATE : GATE + 1] * attn_out[rows, :]
        r2 = lax.rsqrt(jnp.mean(hidden * hidden, axis=1, keepdims=True) + EPS)
        cols[rows, R2 : R2 + 1] = r2
        normed = (hidden * r2 * gains[1:2, :]).astype(BF)
        nm[rows, :] = normed
        nmt[:, rows] = normed.T
        dd[rows, :] = (up[rows, :].astype(F32) * cols[rows, LIVE : LIVE + 1]).astype(BF)


def gelu_both(u):
    k = 0.7978845608028654
    u2 = u * u
    t = jnp.tanh(u * (k + (k * 0.044715) * u2))
    half = 0.5 + 0.5 * t
    act = u * half
    slope = half + act * (1.0 - t) * (k + (3 * k * 0.044715) * u2)
    return act, slope


def mlp_up(nm, dd, wu, wd, act, dup, c, n):
    ff = act.shape[1]
    at = pl.ds(pl.multiple_of(n * 256, 256), 256)
    u = nn(nm[...], flat(wu[c, :, :, :, :, at]))
    dact = nt(dd[...], flat(wd[c, n]))
    a, slope = gelu_both(u)
    act[:, at] = a.astype(BF)
    dup[:, at] = (slope * dact).astype(BF)


def mlp_down(act, wd, down, c):
    @pl.loop(0, down.shape[1] // 256)
    def _(n):
        at = pl.ds(pl.multiple_of(n * 256, 256), 256)
        out = nn(act[...], flat(wd[c, :, :, :, :, at]))
        down[:, at] = out if c == 0 else down[:, at] + out


def mlp_dnormed(dup, wu, dnm, c):
    @pl.loop(0, 2)
    def _(i):
        half = dnm.shape[0] // 2
        rows = pl.ds(pl.multiple_of(i * half, half), half)
        out = nt(dup[rows, :], flat(wu[c]))
        dnm[rows, :] = out if c == 0 else dnm[rows, :] + out


def mlp_grad_down(act, dd, wd, c):
    @pl.loop(0, act.shape[1] // 256)
    def _(n):
        at = pl.ds(pl.multiple_of(n * 256, 256), 256)
        g = tn(act[:, at], dd[...]).astype(BF)
        wd[c, n] = g.reshape(wd.shape[2:])


def mlp_grad_up(nmt, dup, wu, c):
    @pl.loop(0, dup.shape[1] // 256)
    def _(n):
        at = pl.ds(pl.multiple_of(n * 256, 256), 256)
        g = nn(nmt[...], dup[:, at]).astype(BF)
        wu[c, :, :, :, :, at] = g.reshape(wu.shape[1:5] + (256,))


def mid_backward(picked, attn_out, up, down, dnm, gains, cols, datt, new_rows, small, tile=128):
    total = picked.shape[0]
    small[...] = jnp.zeros_like(small)

    @pl.loop(0, total // tile)
    def _(i):
        rows = pl.ds(pl.multiple_of(i * tile, tile), tile)
        x = picked[rows, :].astype(F32)
        gate = cols[rows, GATE : GATE + 1]
        live = cols[rows, LIVE : LIVE + 1]
        r = cols[rows, R2 : R2 + 1]
        ao = attn_out[rows, :]
        branch = gate * ao
        hidden = x + branch
        new_rows[rows, :] = (x + live * (branch + down[rows, :])).astype(BF)
        d = dnm[rows, :]
        hr = hidden * r
        dh = d * hr
        small[1:2, :] += jnp.sum(dh, axis=0, keepdims=True)
        mean = jnp.mean(dh * gains[1:2, :], axis=1, keepdims=True)
        d_hidden = r * (gains[1:2, :] * d - hr * mean)
        dnm[rows, :] = d_hidden
        d_branch = live * up[rows, :].astype(F32) + d_hidden
        d_logit = jnp.sum(d_branch * ao, axis=1, keepdims=True) * gate * (1.0 - gate)
        cols[rows, DLOG : DLOG + 1] = d_logit
        small[2:3, :] += jnp.sum(x * d_logit, axis=0, keepdims=True)
        datt[rows, :] = (d_branch * gate).astype(BF)


def out_backward(datt, mixed, wa, dmix):
    total, width = datt.shape

    @pl.loop(0, 2)
    def _(i):
        half = total // 2
        rows = pl.ds(pl.multiple_of(i * half, half), half)
        dmix[rows, :] = nt(datt[rows, :], flat(wa[3])).astype(BF)

    wa[3] = grad_of(mixed, datt[...]).reshape(wa.shape[1:])


def grad_of(left, right):
    parts = [tn(left[:, n * 384 : n * 384 + 384], right).astype(BF) for n in range(2)]
    return jnp.concatenate(parts, axis=0)


def qkv_backward(dqkv, na, wa, dnorm):
    total, width = na.shape

    @pl.loop(0, 4)
    def _(i):
        half = total // 4
        rows = pl.ds(pl.multiple_of(i * half, half), half)
        dnorm[rows, :] = (
            nt(dqkv[0, rows, :], flat(wa[0]))
            + nt(dqkv[1, rows, :], flat(wa[1]))
            + nt(dqkv[2, rows, :], flat(wa[2]))
        )

    for m in range(3):
        wa[m] = grad_of(na, dqkv[m]).reshape(wa.shape[1:])


def first_backward(picked, up, dnorm, dhid, gains, cols, new_grads, small, tile=128):
    total = picked.shape[0]

    @pl.loop(0, total // tile)
    def _(i):
        rows = pl.ds(pl.multiple_of(i * tile, tile), tile)
        x = picked[rows, :].astype(F32)
        r = cols[rows, R1 : R1 + 1]
        d = dnorm[rows, :]
        xr = x * r
        dx = d * xr
        small[0:1, :] += jnp.sum(dx, axis=0, keepdims=True)
        mean = jnp.mean(dx * gains[0:1, :], axis=1, keepdims=True)
        d_first = r * (gains[0:1, :] * d - xr * mean)
        d_picked = d_first + dhid[rows, :] + cols[rows, DLOG : DLOG + 1] * gains[2:3, :]
        new_grads[rows, :] = (up[rows, :].astype(F32) + d_picked).astype(BF)


def compute_kernel(
    tokens, cot, idx, valid, wa_in, wu_in, wd_in, gains,
    ga, gu, gd, small, new_rows, new_grads,
    wa, wu, wd, picked, up, cols, na, qkv, probs, mixed, attn_out, nm, nmt, dd,
    act, dup, down, dnm, tok_sem, w_sem,
):
    seqs, slots = idx.shape
    width = picked.shape[1]
    scale = (width // HEADS) ** -0.5
    loads = [pltpu.make_async_copy(a, b, w_sem.at[i]) for i, (a, b) in enumerate(((wa_in, wa), (wu_in, wu), (wd_in, wd)))]
    for l in loads:
        l.start()
    pick_phase(tokens, cot, idx, valid, picked, up, cols, (new_rows, new_grads), tok_sem)
    norm_phase(picked, gains, cols, na)
    loads[0].wait()
    qkv_phase(na, wa, qkv, scale)

    @pl.loop(0, seqs)
    def _(s):
        attention_forward(idx, valid, cols, qkv, probs, mixed, s)

    out_phase(mixed, wa, attn_out)
    mid_norm(picked, attn_out, up, gains, cols, nm, nmt, dd, down, dnm)
    loads[1].wait()
    loads[2].wait()
    for c in range(wu.shape[0]):

        @pl.loop(0, 4)
        def _(n):
            mlp_up(nm, dd, wu, wd, act, dup, c, n)

        mlp_down(act, wd, down, c)
        mlp_dnormed(dup, wu, dnm, c)
        mlp_grad_down(act, dd, wd, c)
        mlp_grad_up(nmt, dup, wu, c)
    datt = nm
    dmix = dd
    mid_backward(picked, attn_out, up, down, dnm, gains, cols, datt, new_rows, small)
    out_backward(datt, mixed, wa, dmix)

    @pl.loop(0, seqs)
    def _(s):
        attention_backward(qkv, probs, mixed, dmix, s, slots, scale)

    qkv_backward(qkv, na, wa, down)
    first_backward(picked, up, down, dnm, gains, cols, new_grads, small)
    outs = [pltpu.make_async_copy(a, b, w_sem.at[i]) for i, (a, b) in enumerate(((wa, ga), (wu, gu), (wd, gd)))]
    for o in outs:
        o.start()
    for o in outs:
        o.wait()


MESH_ID = pl.DeviceIdType.MESH
A_MATS, CHUNKS, PLANE = 4, 3, 8


class Place:
    def __init__(self, depth):
        dp = lax.axis_index("dp")
        self.depth = depth
        self.z = lax.axis_index("fsdp")
        self.core = lax.rem(dp, 2)
        self.x = lax.rem(lax.div(dp, 2), 2)
        self.y = lax.rem(lax.div(dp, 4), 2)
        self.sib = (dp + 1 - 2 * self.core, self.z)
        self.xn = (dp + 2 - 4 * self.x, self.z)
        self.yn = (dp + 4 - 8 * self.y, self.z)
        self.dp = dp

    def ahead(self, o):
        return lax.rem(self.z + o, self.depth)

    def behind(self, o):
        return lax.rem(self.z + self.depth - o, self.depth)

    def at_z(self, z):
        return (self.dp, z)

    def greet(self):
        barrier = pltpu.get_barrier_semaphore()
        peers = [self.sib, self.xn, self.yn]
        peers += [self.at_z(self.ahead(o)) for o in range(1, self.depth)]
        for peer in peers:
            pl.semaphore_signal(barrier, inc=1, device_id=peer, device_id_type=MESH_ID)
        pl.semaphore_wait(barrier, len(peers))


def half_of(ref, core):
    width = ref.shape[-1] // 2
    return pl.ds(pl.multiple_of(core * width, 128), width)


class Gather:
    SLOTS = 18

    def __init__(self, me, wa, wu, wd, sends, recvs):
        self.me, self.refs, self.sends, self.recvs = me, (wa, wu, wd), sends, recvs

    def piece(self, a, zi, xi, yi, core):
        wa, wu, wd = self.refs
        if a == 0:
            return wa.at[:, zi, xi, yi, :, half_of(wa, core)]
        ref = wu if a % 2 else wd
        return ref.at[(a - 1) // 2, zi, xi, yi, :, half_of(ref, core)]

    def part(self, a, zi, xi, yi, core, h):
        wa = self.refs[0]
        if a == 0:
            return wa.at[2 * h : 2 * h + 2, zi, xi, yi, :, half_of(wa, core)]
        return self.piece(a, zi, xi, yi, core)

    def ways(self, a):
        return (0, 1) if a == 0 else ((0,) if a % 2 else (1,))

    def copy(self, a, k, ref, dev):
        at = a * self.SLOTS + k
        return pltpu.make_async_remote_copy(
            src_ref=ref, dst_ref=ref, send_sem=self.sends.at[at], recv_sem=self.recvs.at[at],
            device_id=dev, device_id_type=MESH_ID,
        )

    def z_out(self, a, o):
        m = self.me
        return self.copy(a, o, self.piece(a, m.z, m.x, m.y, m.core), m.at_z(m.ahead(o)))

    def x_out(self, a, o):
        m = self.me
        return self.copy(a, 3 + o, self.piece(a, m.behind(o), m.x, m.y, m.core), m.xn)

    def y_out(self, a, o):
        m = self.me
        return self.copy(a, 6 + o, self.piece(a, m.behind(o), m.x, m.y, m.core), m.yn)

    def far_out(self, a, o, h):
        m = self.me
        if h == 0:
            return self.copy(a, 9 + o, self.part(a, m.behind(o), 1 - m.x, m.y, m.core, 0), m.yn)
        return self.copy(a, 12 + o, self.part(a, m.behind(o), m.x, 1 - m.y, m.core, 1), m.xn)

    def core_out(self, a):
        m = self.me
        wa, wu, wd = self.refs
        if a == 0:
            ref = wa.at[:, :, :, :, :, half_of(wa, m.core)]
        else:
            ref = wu if a % 2 else wd
            ref = ref.at[(a - 1) // 2, :, :, :, :, half_of(ref, m.core)]
        return self.copy(a, 0, ref, m.sib)

    def z_in(self, a, o):
        m = self.me
        return self.copy(a, o, self.piece(a, m.behind(o), m.x, m.y, m.core), m.at_z(m.behind(o)))

    def x_in(self, a, o):
        m = self.me
        return self.copy(a, 3 + o, self.piece(a, m.behind(o), 1 - m.x, m.y, m.core), m.xn)

    def y_in(self, a, o):
        m = self.me
        return self.copy(a, 6 + o, self.piece(a, m.behind(o), m.x, 1 - m.y, m.core), m.yn)

    def far_in(self, a, o, h):
        m = self.me
        part = self.part(a, m.behind(o), 1 - m.x, 1 - m.y, m.core, h)
        return self.copy(a, (9 if h == 0 else 12) + o, part, m.yn if h == 0 else m.xn)

    def core_in(self, a):
        m = self.me
        wa, wu, wd = self.refs
        if a == 0:
            ref = wa.at[:, :, :, :, :, half_of(wa, 1 - m.core)]
        else:
            ref = wu if a % 2 else wd
            ref = ref.at[(a - 1) // 2, :, :, :, :, half_of(ref, 1 - m.core)]
        return self.copy(a, 0, ref, m.sib)

    def origins(self):
        return range(1, self.me.depth)

    def send_z(self, a):
        for o in self.origins():
            self.z_out(a, o).start()

    def spread(self, a, o):
        self.z_in(a, o).wait_recv()
        self.x_out(a, o).start()
        self.y_out(a, o).start()

    def forward(self, a, o):
        self.x_in(a, o).wait_recv()
        if 0 in self.ways(a):
            self.far_out(a, o, 0).start()
        self.y_in(a, o).wait_recv()
        if 1 in self.ways(a):
            self.far_out(a, o, 1).start()

    def across(self, a):
        for o in self.origins():
            for h in self.ways(a):
                self.far_in(a, o, h).wait_recv()
        self.core_out(a).start()

    def ready(self, a):
        self.core_in(a).wait_recv()

    def settle(self, a):
        for o in self.origins():
            self.z_out(a, o).wait_send()
            self.x_out(a, o).wait_send()
            self.y_out(a, o).wait_send()
            for h in self.ways(a):
                self.far_out(a, o, h).wait_send()
        self.core_out(a).wait_send()


class Owned:
    def __init__(self, me, shards, wa, wu, wd, sems):
        wq, wk, wv, wo, up, down = shards
        z, core = me.z, me.core
        half = half_of(wa, core)
        self.copies = {0: [], 1: [], 2: [], 3: [], 4: [], 5: [], 6: []}
        for m, w in enumerate((wq, wk, wv, wo)):
            self.copies[0].append((w.at[:, :, :, half], wa.at[m, z, :, :, :, half]))
        ff_own = up.shape[-1] // me.depth
        for c in range(CHUNKS):
            for j in range(2):
                block = 2 * core + j
                src = up.at[:, :, :, pl.ds(pl.multiple_of(block * ff_own + c * 256, 128), 256)]
                dst = wu.at[c, z, :, :, :, pl.ds(pl.multiple_of(block * 256, 128), 256)]
                self.copies[1 + 2 * c].append((src, dst))
            self.copies[2 + 2 * c].append((down.at[c, :, :, :, half], wd.at[c, z, :, :, :, half]))
        self.sems = sems

    def all_of(self, a):
        base = sum(len(self.copies[b]) for b in range(a))
        for i, (src, dst) in enumerate(self.copies[a]):
            yield pltpu.make_async_copy(src, dst, self.sems.at[base + i])

    def start(self, a):
        for c in self.all_of(a):
            c.start()

    def wait(self, a):
        for c in self.all_of(a):
            c.wait()


class Reduce:
    SLOTS = 14

    def __init__(
        self, me, w, from_core, from_x, from_y, then_x, then_y, from_z, sends, recvs, frees, at, way
    ):
        self.me, self.w, self.way, self.free, base = me, w, way, frees.at[at], at * self.SLOTS
        self.from_core, self.from_x, self.from_y = from_core, from_x, from_y
        self.then_x, self.then_y, self.from_z = then_x, then_y, from_z
        self.sends, self.recvs, self.base = sends, recvs, base
        self.mine, self.theirs = half_of(w, me.core), half_of(w, 1 - me.core)

    def copy(self, k, src, dst, dev):
        at = self.base + k
        return pltpu.make_async_remote_copy(
            src_ref=src, dst_ref=dst, send_sem=self.sends.at[at], recv_sem=self.recvs.at[at],
            device_id=dev, device_id_type=MESH_ID,
        )

    def core_copy(self):
        return self.copy(0, self.w.at[:, :, :, :, self.theirs], self.from_core, self.me.sib)

    def plane_first(self):
        m, w = self.me, self.w
        return (
            self.copy(1, w.at[0:2, 1 - m.x, :, :, self.mine], self.from_x, m.xn),
            self.copy(2, w.at[2:4, :, 1 - m.y, :, self.mine], self.from_y, m.yn),
        )

    def plane_second(self):
        m, w = self.me, self.w
        return (
            self.copy(3, w.at[0:2, m.x, 1 - m.y, :, self.mine], self.then_y, m.yn),
            self.copy(4, w.at[2:4, 1 - m.x, m.y, :, self.mine], self.then_x, m.xn),
        )

    def z_copy(self, o):
        m = self.me
        src = self.w.at[m.ahead(o), m.x, m.y, :, self.mine]
        return self.copy(4 + o, src, self.from_z.at[o - 1], m.at_z(m.ahead(o)))

    def back(self, k, xi, yi, dev):
        ref = self.from_core.at[0, xi, yi]
        return self.copy(k, ref, ref, dev)

    def core_back(self):
        return self.copy(11, self.from_core.at[0], self.from_core.at[1], self.me.sib)

    def add(self, at, arrived):
        self.w[at] = (self.w[at].astype(F32) + arrived.astype(F32)).astype(BF)

    def t1(self):
        self.core_copy().start()

    def t2(self):
        m = self.me
        self.core_copy().wait()

        @pl.loop(0, 2 * m.depth)
        def _(i):
            zi, xi = lax.div(i, 2), lax.rem(i, 2)
            self.add((zi, xi, slice(None), slice(None), self.mine), self.from_core[zi, xi])

        pl.semaphore_signal(self.free, inc=1, device_id=m.sib, device_id_type=MESH_ID)
        for c in self.plane_first():
            c.start()

    def t3(self):
        m = self.me
        first = self.plane_first()
        first[0].wait()
        for zi in range(2):
            self.add((zi, m.x, slice(None), slice(None), self.mine), self.from_x[zi])
        first[1].wait()
        for zi in range(2):
            self.add((2 + zi, slice(None), m.y, slice(None), self.mine), self.from_y[zi])
        for c in self.plane_second():
            c.start()

    def t4(self):
        m = self.me
        second = self.plane_second()
        second[0].wait()
        self.add((slice(0, 2), m.x, m.y, slice(None), self.mine), self.then_y[...])
        second[1].wait()
        self.add((slice(2, 4), m.x, m.y, slice(None), self.mine), self.then_x[...])
        for o in range(1, m.depth):
            self.z_copy(o).start()

    def t5(self):
        m = self.me
        at = (m.z, m.x, m.y, slice(None), self.mine)
        total = self.w[at].astype(F32)
        for o in range(1, m.depth):
            self.z_copy(o).wait()
            total = total + self.from_z[o - 1].astype(F32)
        self.from_core[0, m.x, m.y] = total.astype(BF)
        self.back(8, m.x, m.y, m.xn).start()
        self.back(9, m.x, m.y, m.yn).start()

    def far(self):
        m = self.me
        if self.way == 0:
            return self.back(10, 1 - m.x, m.y, m.yn)
        return self.back(10, m.x, 1 - m.y, m.xn)

    def t6(self):
        m = self.me
        self.back(8, 1 - m.x, m.y, m.xn).wait_recv()
        self.back(9, m.x, 1 - m.y, m.yn).wait_recv()
        self.far().start()

    def t7(self):
        m = self.me
        self.back(10, 1 - m.x, 1 - m.y, m.yn if self.way == 0 else m.xn).wait_recv()
        pl.semaphore_wait(self.free, 1)
        self.core_back().start()

    def t8(self):
        m = self.me
        self.core_back().wait()
        self.back(8, m.x, m.y, m.xn).wait_send()
        self.back(9, m.x, m.y, m.yn).wait_send()
        self.far().wait_send()


class SmallSum:
    def __init__(self, me, small, inbox, sends, recvs, base):
        self.me, self.small, self.inbox = me, small, inbox
        self.sends, self.recvs, self.base = sends, recvs, base

    def copy(self, k, dev):
        return pltpu.make_async_remote_copy(
            src_ref=self.small.at[k], dst_ref=self.inbox.at[k],
            send_sem=self.sends.at[self.base + k], recv_sem=self.recvs.at[self.base + k],
            device_id=dev, device_id_type=MESH_ID,
        )

    def peer(self, k):
        return (self.me.sib, self.me.xn, self.me.yn)[k]

    def step(self, k):
        m = self.me
        if 1 <= k <= 3:
            self.copy(k - 1, self.peer(k - 1)).wait()
            self.small[k] = self.small[k - 1] + self.inbox[k - 1]
        if k <= 2:
            self.copy(k, self.peer(k)).start()
        if k == 3:
            for o in range(1, m.depth):
                self.z_copy(o).start()
        if k == 4:
            total = self.small[3]
            for o in range(1, m.depth):
                self.z_copy(o).wait()
                total = total + self.inbox[2 + o]
            self.small[4] = total

    def z_copy(self, o):
        m = self.me
        at = self.base + 2 + o
        return pltpu.make_async_remote_copy(
            src_ref=self.small.at[3], dst_ref=self.inbox.at[2 + o],
            send_sem=self.sends.at[at], recv_sem=self.recvs.at[at],
            device_id=m.at_z(m.ahead(o)), device_id_type=MESH_ID,
        )


def gather_kernel(depth, wq, wk, wv, wo, up, down, gpad, wa_out, wu_out, wd_out, gains_out,
                  wa, wu, wd, gbox, own_sem, sends, recvs):
    me = Place(depth)
    me.greet()
    own = Owned(me, (wq, wk, wv, wo, up, down), wa, wu, wd, own_sem)
    ag = Gather(me, wa, wu, wd, sends, recvs)
    arrays = range(7)
    gsem = 7 * Gather.SLOTS
    def gcopy(o):
        return pltpu.make_async_remote_copy(
            src_ref=gpad, dst_ref=gbox.at[o - 1], send_sem=sends.at[gsem + o], recv_sem=recvs.at[gsem + o],
            device_id=me.at_z(me.ahead(o)), device_id_type=MESH_ID)
    for o in range(1, depth):
        gcopy(o).start()
    for a in arrays:
        own.start(a)
    for a in arrays:
        own.wait(a)
        ag.send_z(a)
    for t in range(len(arrays) + 3):
        if t < 7:
            for o in range(1, depth):
                ag.spread(t, o)
        if 0 <= t - 1 < 7:
            for o in range(1, depth):
                ag.forward(t - 1, o)
        if 0 <= t - 2 < 7:
            ag.across(t - 2)
        if 0 <= t - 3 < 7:
            ag.ready(t - 3)
    total = gpad[...].astype(F32)
    for o in range(1, depth):
        gcopy(o).wait()
        total = total + gbox[o - 1].astype(F32)
    gains_out[...] = total[:8]
    for a in arrays:
        ag.settle(a)
    outs = [pltpu.make_async_copy(a, b, own_sem.at[i]) for i, (a, b) in enumerate(((wa, wa_out), (wu, wu_out), (wd, wd_out)))]
    for o in outs:
        o.start()
    for o in outs:
        o.wait()


def reduce_scratch(total_depth, rows_a, width, rows_d, ff_c):
    def boxes(n, rows, cols):
        v = lambda *s: pltpu.VMEM((n,) + s + (rows, cols), BF)
        return [v(4, 2, 2), v(2, 2), v(2, 2), v(2), v(2), v(3)]
    return boxes(4, rows_a, width // 2) + boxes(3, rows_a, ff_c // 2) + boxes(3, rows_d, width // 2)


def reducers(me, wa, wu, wd, boxes, sends, recvs, frees):
    out = []
    for w, b, ways in ((wa, boxes[0:6], (0, 1, 0, 1)), (wu, boxes[6:12], (0, 0, 0)), (wd, boxes[12:18], (1, 1, 1))):
        for i, way in enumerate(ways):
            out.append(Reduce(me, w.at[i], *[x.at[i] for x in b], sends, recvs, frees, len(out), way))
    return out


def reduce_kernel(depth, ga, gu, gd, small_in, fa, fu, fd, small_out,
                  wa, wu, wd, small, inbox, load_sem, sends, recvs, frees, *boxes):
    me = Place(depth)
    me.greet()
    loads = [pltpu.make_async_copy(a, b, load_sem.at[i]) for i, (a, b) in enumerate(((ga, wa), (gu, wu), (gd, wd)))]
    for l in loads:
        l.start()
    for l in loads:
        l.wait()
    rs = reducers(me, wa, wu, wd, boxes, sends, recvs, frees)
    order = [4, 7, 5, 8, 6, 9, 3, 0, 1, 2]
    ss = SmallSum(me, small, inbox, sends, recvs, 10 * Reduce.SLOTS)
    small[0] = small_in[...]
    steps = ("t1", "t2", "t3", "t4", "t5", "t6", "t7", "t8")
    for t in range(len(order) + len(steps) - 1):
        for k in range(len(steps)):
            if 0 <= t - k < len(order):
                getattr(rs[order[t - k]], steps[k])()
    for k in range(5):
        ss.step(k)
    small_out[...] = small[4]
    outs = []
    for box, dst in ((boxes[0], fa), (boxes[6], fu), (boxes[12], fd)):
        for h, core in ((0, me.core), (1, 1 - me.core)):
            outs.append(pltpu.make_async_copy(box.at[:, h], dst.at[:, :, :, :, half_of(dst, core)], load_sem.at[len(outs)]))
    for o in outs:
        o.start()
    for o in outs:
        o.wait()


def place_kernel(idx, tokens, cot, new_rows, new_grads, fa, fu, fd,
                 out, grad, gq, gk, gv, go, gup, gdown):
    s = pl.program_id(0)
    length, slots = tokens.shape[0], idx.shape[1]
    spot = lax.broadcasted_iota(jnp.int32, (length, slots), 0)
    hot = jnp.where(spot == idx[pl.ds(s, 1), :], 1.0, 0.0)
    hit = jnp.sum(hot, axis=1, keepdims=True) > 0
    hot = hot.astype(BF)
    for src, rows, dst in ((tokens, new_rows, out), (cot, new_grads, grad)):
        dst[...] = jnp.where(hit, nn(hot, rows[...]), src[...].astype(F32)).astype(BF)
    for m, g in enumerate((gq, gk, gv, go)):
        g[...] = fa[m, 0].astype(F32)
    quarter = 256
    ff_own = gup.shape[1] // 4
    for c in range(CHUNKS):
        for j in range(4):
            gup[:, j * ff_own + c * quarter : j * ff_own + (c + 1) * quarter] = fu[c, 0, :, j * quarter : (j + 1) * quarter].astype(F32)
        gdown[c, 0] = fd[c, 0].astype(F32)


def remote_params(collective_id, limit=60):
    return pltpu.CompilerParams(
        collective_id=collective_id, has_side_effects=True, vmem_limit_bytes=limit * 2**20
    )


def over_groups(groups, terms):
    if groups == 1:
        return terms
    dp = groups * PLANE
    total = [t.astype(F32) for t in terms]
    for k in range(groups.bit_length() - 1):
        hop = PLANE << k
        pairs = [(i, i ^ hop) for i in range(dp)]
        total = [t + lax.ppermute(t, "dp", pairs) for t in total]
    return total


def body(depth, groups, tokens, row_index, row_valid, w_query, w_key, w_value, w_out, w_up, w_down,
         gain_attn, gain_mlp, w_router, cotangent):
    seqs, slots = row_index.shape
    width = tokens.shape[1]
    own = w_query.shape[0]
    ff = w_up.shape[1]
    length = tokens.shape[0] // seqs
    total = seqs * slots
    rq, cw = own // 4, ff // CHUNKS
    dq = w_down.shape[0] // (4 * CHUNKS)
    sd = jax.ShapeDtypeStruct
    hbm, vm = pl.BlockSpec(memory_space=pl.ANY), pl.BlockSpec(memory_space=pltpu.VMEM)
    sem = pltpu.SemaphoreType.DMA
    vmem = pltpu.VMEM
    z = lax.axis_index("fsdp")
    gains3 = jnp.stack([gain_attn, gain_mlp, w_router])
    gpad = lax.dynamic_update_slice(jnp.zeros((16, width), BF), gains3, (0, z * own))
    squares = [w.reshape(2, 2, rq, width) for w in (w_query, w_key, w_value, w_out)]
    sa, su, sdn = (A_MATS, depth, 2, 2, rq, width), (CHUNKS, depth, 2, 2, rq, cw), (CHUNKS, depth, 2, 2, dq, width)
    nag = 7 * Gather.SLOTS + 8
    wa, wu, wd, gains = pl.pallas_call(
        functools.partial(gather_kernel, depth),
        out_shape=(sd(sa, BF), sd(su, BF), sd(sdn, BF), sd((8, width), F32)),
        in_specs=[hbm] * 6 + [vm], out_specs=(hbm, hbm, hbm, vm),
        scratch_shapes=[vmem(sa, BF), vmem(su, BF), vmem(sdn, BF), vmem((depth - 1, 16, width), BF), sem((16,)), sem((nag,)), sem((nag,))],
        compiler_params=remote_params(0),
    )(*squares, w_up.reshape(2, 2, rq, ff), w_down.reshape(CHUNKS, 2, 2, dq, width), gpad)
    rows = (total, width)
    ga, gu, gd, small, new_rows, new_grads = pl.pallas_call(
        compute_kernel,
        out_shape=(sd(sa, BF), sd(su, BF), sd(sdn, BF), sd((8, width), F32), sd(rows, BF), sd(rows, BF)),
        in_specs=[hbm, hbm, vm, vm, hbm, hbm, hbm, vm], out_specs=(hbm, hbm, hbm, vm, vm, vm),
        scratch_shapes=[
            vmem(sa, BF), vmem(su, BF), vmem(sdn, BF), vmem(rows, BF), vmem(rows, BF), vmem((total, 128), F32),
            vmem(rows, BF), vmem((3,) + rows, BF), vmem((seqs * width // 128, 2 * slots, slots), BF), vmem(rows, BF),
            vmem(rows, F32), vmem(rows, BF), vmem((width, total), BF), vmem(rows, BF), vmem((total, cw), BF),
            vmem((total, cw), BF), vmem(rows, F32), vmem(rows, F32), sem((2,)), sem((3,)),
        ],
        compiler_params=pltpu.CompilerParams(vmem_limit_bytes=60 * 2**20),
    )(tokens, cotangent, row_index, row_valid, wa, wu, wd, gains)
    nrs = 10 * Reduce.SLOTS + 8
    fa, fu, fd, sums = pl.pallas_call(
        functools.partial(reduce_kernel, depth),
        out_shape=(sd(sa[:1] + sa[2:], BF), sd(su[:1] + su[2:], BF), sd(sdn[:1] + sdn[2:], BF), sd((8, width), F32)),
        in_specs=[hbm, hbm, hbm, vm], out_specs=(hbm, hbm, hbm, vm),
        scratch_shapes=[vmem(sa, BF), vmem(su, BF), vmem(sdn, BF), vmem((5, 8, width), F32), vmem((2 + depth, 8, width), F32),
                        sem((6,)), sem((nrs,)), sem((nrs,)), pltpu.SemaphoreType.REGULAR((10,))] + reduce_scratch(depth, rq, width, dq, cw),
        compiler_params=remote_params(1),
    )(ga, gu, gd, small)
    fa, fu, fd, sums = over_groups(groups, (fa, fu, fd, sums))
    out, grad, gq, gk, gv, go, gup, gdown = pl.pallas_call(
        place_kernel,
        grid=(seqs,),
        out_shape=(sd(tokens.shape, BF), sd(tokens.shape, BF)) + (sd((own, width), F32),) * 4 + (sd((own, ff), F32), sd((CHUNKS, 4, dq, width), F32)),
        in_specs=[pl.BlockSpec((seqs, slots), lambda s: (0, 0))] + [pl.BlockSpec((length, width), lambda s: (s, 0))] * 2
        + [pl.BlockSpec((slots, width), lambda s: (s, 0))] * 2
        + [pl.BlockSpec((A_MATS, 1, rq, width), lambda s: (0, s, 0, 0)), pl.BlockSpec((CHUNKS, 1, rq, cw), lambda s: (0, s, 0, 0)), pl.BlockSpec((CHUNKS, 1, dq, width), lambda s: (0, s, 0, 0))],
        out_specs=[pl.BlockSpec((length, width), lambda s: (s, 0))] * 2 + [pl.BlockSpec((rq, width), lambda s: (s, 0))] * 4
        + [pl.BlockSpec((rq, ff), lambda s: (s, 0)), pl.BlockSpec((CHUNKS, 1, dq, width), lambda s: (0, s, 0, 0))],
        compiler_params=pltpu.CompilerParams(vmem_limit_bytes=50 * 2**20),
    )(row_index, tokens, cotangent, new_rows, new_grads, fa.reshape(A_MATS, 4, rq, width), fu.reshape(CHUNKS, 4, rq, cw), fd.reshape(CHUNKS, 4, dq, width))
    vec = lax.dynamic_slice(sums, (0, z * own), (3, own))
    return (out, grad, gq, gk, gv, go, gup, gdown.reshape(w_down.shape), vec[0], vec[1], vec[2])


def solution(mesh):
    depth = mesh.shape["fsdp"]
    both = P(("dp", "fsdp"), None)
    weight, vector = P("fsdp", None), P("fsdp")
    return jax.shard_map(
        functools.partial(body, depth, mesh.shape["dp"] // PLANE),
        mesh=mesh,
        in_specs=(both,) * 3 + (weight,) * 6 + (vector,) * 3 + (both,),
        out_specs=(both, both) + (weight,) * 6 + (vector,) * 3,
        check_vma=False,
    )
```

time: 1300 us -> 319 us (0.25)
  waiting for transfers between devices: 637 us -> 0 us
  other arithmetic: 324 us -> 0.01 us
  Pallas kernels: 0 us -> 309 us
  matrix products: 158 us -> 0 us
  local copies, waits for them, and re-layouts: 107 us -> 8.33 us
  blocking collectives: 44.6 us -> 0 us
  between operations: 17.3 us -> 0.72 us
    reduce_scatter x6 -> x0, waiting for transfers between devices: 435 us -> none  [body(): summed = lax.psum_scatter(summed, 'fsdp', scatter_dimension=0, tiled=True)]
    pallas_call x0 -> x4, Pallas kernels: none -> 309 us  [the longest x1 110 us: body(): pl.pallas_call(functools.partial(reduce_kernel, depth), out_shape=(sd(sa[...]
    scatter-add x4 -> x0, other arithmetic: 277 us -> none  [put_rows(): seq_rows.at[seq_index].add(seq_add)]
    all_gather x6 -> x0, waiting for transfers between devices: 198 us -> none  [the longest x1 86.4 us: body(): lax.all_gather(shards[5], 'fsdp', axis=0, tiled=True)]
    dot_general x52 -> x0, matrix products: 158 us -> none  [the longest x14 58.1 us: rows_by(): return jnp.dot(left_mat, right_mat, preferred_element_type=jnp.float32)]
    unnamed x2 -> x0, blocking collectives: 32.2 us -> none
    gather x4 -> x0, local copies, waits for them, and re-layouts: 32 us -> none  [pick_rows(): jnp.take(seq_rows, seq_index, axis=0)]
    unnamed x271 -> x10, local copies, waits for them, and re-layouts: 33.8 us -> 4.41 us
  transfers between devices with their start and end apart: 13 -> 0, of which waited for: 9 -> 0; matrix products, arithmetic and copies ran while one was open for 36% -> 0% of each run, Pallas kernels for 0% -> 0%
where the time goes in v1:
time: 319 us; the launch traced here: 318 us
  Pallas kernels  309 us (97%)
  local copies, waits for them, and re-layouts  8.33 us (3%)
    pallas_call x1, Pallas kernels, body(): pl.pallas_call(functools.partial(reduce_kernel, depth), out_shape=(sd(sa[...  110 us
    pallas_call x1, Pallas kernels, body(): pl.pallas_call(compute_kernel, out_shape=(sd(sa, BF), sd(su, BF), sd(sdn,...  108 us
    pallas_call x1, Pallas kernels, body(): pl.pallas_call(functools.partial(gather_kernel, depth), out_shape=(sd(sa,...  77.3 us
    pallas_call x1, Pallas kernels, body(): pl.pallas_call(place_kernel, grid=(seqs,), out_shape=(sd(tokens.shape, BF...  12.9 us

profile of v1, /device:TPU:0, one launch (start us, length us, event | category | flops | bytes accessed | tf_op | source)
XLA Modules:
  0.0 318.1 jit_solution(16492931495714049966)
XLA Ops:
  0.6 0.7 stack.12
  1.3 0.7 stack.13
  2.0 0.7 stack.14
  2.6 0.5 dynamic_update_slice.3.gpad
  3.1 0.0 copy-start.4
  3.1 0.6 copy-done.4
  3.7 77.3 %shard_map.212 = (bf16[4,4,2,2,48,768]{5,4,3,2,1,0:T(8,128)(2,1)}, bf16[3,4,2,2,48,1024]{5,4,3,2,1,0:T(8,128)(2,1)}, bf16[3,4,2,2,64,768]{5,4,3,2,1,0:T(8,128)(2,1)}, f32[8,768]{1,0:T(8,128)}) custom-call(bf16[2,2,48,768]{3,2,1,0:T(8,128)(2,1)} %bitcast.18, bf16[2,2,48,768]{3,2,1,0:T(8,128)(2,1)} %bitcast.19, bf16[2,2,48,768]{3,2,1,0:T(8,128)(2,1)} %bitcast.20, ...), custom_call_target="tpu_custom_call" | custom-call | tf_op jit(solution)/shard_map/pallas_call | solution.py:861
  81.1 108.3 %shard_map.213 = (bf16[4,4,2,2,48,768]{5,4,3,2,1,0:T(8,128)(2,1)}, bf16[3,4,2,2,48,1024]{5,4,3,2,1,0:T(8,128)(2,1)}, bf16[3,4,2,2,64,768]{5,4,3,2,1,0:T(8,128)(2...) custom-call(bf16[4096,768]{1,0:T(8,128)(2,1)} %tokens.3, bf16[4096,768]{1,0:T(8,128)(2,1)} %cot.3, ...), custom_call_target="tpu_custom_call" | custom-call | tf_op jit(solution)/shard_map/pallas_call | solution.py:869
  189.4 0.0 copy-start.3
  189.4 110.5 %shard_map.214 = (bf16[4,2,2,48,768]{4,3,2,1,0:T(8,128)(2,1)}, bf16[3,2,2,48,1024]{4,3,2,1,0:T(8,128)(2,1)}, bf16[3,2,2,64,768]{4,3,2,1,0:T(8,128)(2,1)}, f32[8,768]{1,0:T(8,128)}) custom-call(bf16[4,4,2,2,48,768]{5,4,3,2,1,0:T(8,128)(2,1)} %get-tuple-element.39.ga, bf16[3,4,2,2,48,1024]{5,4,3,2,1,0:T(8,128)(2,1)} %get-tuple-element.40.gu, ...), custom_call_target="tpu_custom_call" | custom-call | tf_op jit(solution)/shard_map/pallas_call | solution.py:882
  299.8 0.0 copy-done.3
  299.9 0.0 copy-start
  299.9 1.3 copy-done
  301.1 0.0 copy-start.1
  301.1 1.3 copy-done.1
  302.4 0.0 copy-start.2
  302.4 1.3 copy-done.2
  303.7 12.9 %shard_map.215 = (bf16[4096,768]{1,0:T(8,128)(2,1)}, bf16[4096,768]{1,0:T(8,128)(2,1)}, f32[192,768]{1,0:T(8,128)}, f32[192,768]{1,0:T(8,128)}, f32[192,768]{1,0...) custom-call(s32[4,256]{1,0:T(4,128)S(1)} %copy-done.3, bf16[4096,768]{1,0:T(8,128)(2,1)} %tokens.3, ...), custom_call_target="tpu_custom_call" | custom-call | tf_op jit(solution)/shard_map/pallas_call | solution.py:891
  316.6 1.5 fusion
  (2 shorter events, 0.0 us)
Async XLA Ops:
  3.1 0.6 copy-start.4
  189.4 110.5 %copy-start.3 = (s32[4,256]{1,0:T(4,128)S(1)}, s32[4,256]{1,0:T(4,128)}, u32[]{:S(2)}) copy-start(s32[4,256]{1,0:T(4,128)} %idx.3) | copy-start | bytes 12292
  299.9 1.3 copy-start
  301.1 1.3 copy-start.1
  302.4 1.3 copy-start.2

commit v2 on v1

--- a/solution.py
+++ b/solution.py
@@ -32,35 +32,40 @@
     return v.reshape(-1, v.shape[-1])
 
 
-def pick_phase(tokens, cot, idx, valid, picked, up, cols, tok_buf, tok_sem):
-    seqs, slots = idx.shape
-    length = tokens.shape[0] // seqs
-
-    def fetch(t, slot):
-        src = tokens if t % 2 == 0 else cot
-        return pltpu.make_async_copy(
-            src.at[pl.ds((t // 2) * length, length)], tok_buf[slot], tok_sem.at[slot]
-        )
-
-    fetch(0, 0).start()
-    fetch(1, 1).start()
-    pad = jnp.zeros((8 - seqs, slots), F32) if seqs < 8 else None
-    for what, k in ((idx, POS), (valid, LIVE)):
-        rows8 = what[...].astype(F32)
-        if pad is not None:
-            rows8 = jnp.concatenate([rows8, pad], axis=0)
-        turned = rows8.T
-        for s in range(seqs):
-            cols[s * slots : (s + 1) * slots, k : k + 1] = turned[:, s : s + 1]
-    lane = lax.broadcasted_iota(jnp.int32, (slots, length), 1).astype(F32)
-    for s in range(seqs):
+class Picker:
+    def __init__(self, tokens, cot, picked, up, cols, bufs, sems):
+        self.srcs, self.dsts, self.cols, self.bufs, self.sems = (tokens, cot), (picked, up), cols, bufs, sems
+
+    def fetch(self, s, b):
+        width = self.srcs[b].shape[-1]
+        dst = self.bufs[b].at[:, :, :, :, 0:width]
+        return pltpu.make_async_copy(self.srcs[b].at[s], dst, self.sems.at[b])
+
+    def start(self, s):
+        for b in range(2):
+            self.fetch(s, b).start()
+
+    def turn(self, idx, valid):
+        seqs, slots = idx.shape
+        for what, k in ((idx, POS), (valid, LIVE)):
+            rows8 = what[...].astype(F32)
+            if seqs < 8:
+                rows8 = jnp.concatenate([rows8, jnp.zeros((8 - seqs, slots), F32)], axis=0)
+            turned = rows8.T
+            for s in range(seqs):
+                self.cols[s * slots : (s + 1) * slots, k : k + 1] = turned[:, s : s + 1]
+
+    def pick(self, s, slots, more):
+        width = self.srcs[0].shape[-1]
         rows = slice(s * slots, (s + 1) * slots)
-        hot = jnp.where(lane == cols[rows, POS : POS + 1], 1.0, 0.0).astype(BF)
-        for b, dst in ((0, picked), (1, up)):
-            fetch(2 * s + b, b).wait()
-            dst[rows, :] = nn(hot, tok_buf[b][...]).astype(BF)
-            if s + 1 < seqs:
-                fetch(2 * s + 2 + b, b).start()
+        length = self.bufs[0].shape[0] * self.bufs[0].shape[1] * self.bufs[0].shape[2] * self.bufs[0].shape[3]
+        lane = lax.broadcasted_iota(jnp.int32, (slots, length), 1).astype(F32)
+        hot = jnp.where(lane == self.cols[rows, POS : POS + 1], 1.0, 0.0).astype(BF)
+        for b in range(2):
+            self.fetch(s, b).wait()
+            self.dsts[b][rows, :] = nn(hot, flat(self.bufs[b][:, :, :, :, 0:width])).astype(BF)
+            if more:
+                self.fetch(s + 1, b).start()
 
 
 def norm_phase(picked, gains, cols, na, tile=256):
@@ -78,6 +83,14 @@
         na[rows, :] = (x * r1 * gains[0:1, :]).astype(BF)
 
 
+def norm_again(picked, gains, cols, na, tile=256):
+    @pl.loop(0, picked.shape[0] // tile)
+    def _(i):
+        rows = pl.ds(pl.multiple_of(i * tile, tile), tile)
+        x = picked[rows, :].astype(F32)
+        na[rows, :] = (x * cols[rows, R1 : R1 + 1] * gains[0:1, :]).astype(BF)
+
+
 def qkv_phase(na, wa, qkv, scale):
     width = na.shape[1]
     for m in range(3):
@@ -94,6 +107,11 @@
 def two_heads(v2, low_half):
     zero = jnp.zeros_like(v2)
     return jnp.concatenate([jnp.where(low_half, v2, zero), jnp.where(low_half, zero, v2)], axis=0)
+
+
+def prob_spot(s, p, slots):
+    at = pl.ds(pl.multiple_of(s * slots, slots), slots)
+    return (p // 2, slice(2 * (p % 2), 2 * (p % 2) + 2), slice(None), slice(None), slice(None), at)
 
 
 def attention_forward(idx, valid, cols, qkv, probs, mixed, s):
@@ -112,7 +130,8 @@
         scores = nt(q2, qkv[1, rows, at]) + bias
         e = jnp.exp(scores - jnp.max(scores, axis=1, keepdims=True))
         pr = (e * (1.0 / jnp.sum(e, axis=1, keepdims=True))).astype(BF)
-        probs[s * (width // 128) + p] = pr
+        spot = prob_spot(s, p, slots)
+        probs[spot] = pr.reshape(2, 2, 2, 64, slots)
         o = nn(pr, qkv[2, rows, at])
         mixed[rows, at] = jnp.where(low_half, o[:slots], o[slots:]).astype(BF)
 
@@ -129,7 +148,7 @@
         delta = jnp.sum(do2.astype(F32) * o2, axis=1, keepdims=True)
         k2 = qkv[1, rows, at]
         dp = nt(do2, qkv[2, rows, at])
-        pr = probs[s * (width // 128) + p]
+        pr = flat(probs[prob_spot(s, p, slots)])
         ds = (pr.astype(F32) * (dp - delta)).astype(BF)
         q2 = two_heads(qkv[0, rows, at], low_half)
         dq = nn(ds, k2) * scale
@@ -147,7 +166,7 @@
         attn_out[:, at] = nn(mixed[...], flat(wa[3, :, :, :, :, at]))
 
 
-def mid_norm(picked, attn_out, up, gains, cols, nm, nmt, dd, down, dnm, tile=256):
+def mid_norm(picked, attn_out, up, gains, cols, nm, nmt, dd, tile=256):
     total = picked.shape[0]
     for i in range(total // tile):
         rows = slice(i * tile, (i + 1) * tile)
@@ -171,20 +190,20 @@
 
 
 def mlp_up(nm, dd, wu, wd, act, dup, c, n):
-    ff = act.shape[1]
     at = pl.ds(pl.multiple_of(n * 256, 256), 256)
     u = nn(nm[...], flat(wu[c, :, :, :, :, at]))
     dact = nt(dd[...], flat(wd[c, n]))
     a, slope = gelu_both(u)
-    act[:, at] = a.astype(BF)
-    dup[:, at] = (slope * dact).astype(BF)
+    shape = act.shape[:4] + (256,)
+    act[:, :, :, :, at] = a.astype(BF).reshape(shape)
+    dup[:, :, :, :, at] = (slope * dact).astype(BF).reshape(shape)
 
 
 def mlp_down(act, wd, down, c):
     @pl.loop(0, down.shape[1] // 256)
     def _(n):
         at = pl.ds(pl.multiple_of(n * 256, 256), 256)
-        out = nn(act[...], flat(wd[c, :, :, :, :, at]))
+        out = nn(flat(act[...]), flat(wd[c, :, :, :, :, at]))
         down[:, at] = out if c == 0 else down[:, at] + out
 
 
@@ -193,23 +212,23 @@
     def _(i):
         half = dnm.shape[0] // 2
         rows = pl.ds(pl.multiple_of(i * half, half), half)
-        out = nt(dup[rows, :], flat(wu[c]))
+        out = nt(flat(dup[pl.ds(2 * i, 2)]), flat(wu[c]))
         dnm[rows, :] = out if c == 0 else dnm[rows, :] + out
 
 
 def mlp_grad_down(act, dd, wd, c):
-    @pl.loop(0, act.shape[1] // 256)
+    @pl.loop(0, act.shape[-1] // 256)
     def _(n):
         at = pl.ds(pl.multiple_of(n * 256, 256), 256)
-        g = tn(act[:, at], dd[...]).astype(BF)
+        g = tn(flat(act[:, :, :, :, at]), dd[...]).astype(BF)
         wd[c, n] = g.reshape(wd.shape[2:])
 
 
 def mlp_grad_up(nmt, dup, wu, c):
-    @pl.loop(0, dup.shape[1] // 256)
+    @pl.loop(0, dup.shape[-1] // 256)
     def _(n):
         at = pl.ds(pl.multiple_of(n * 256, 256), 256)
-        g = nn(nmt[...], dup[:, at]).astype(BF)
+        g = nn(nmt[...], flat(dup[:, :, :, :, at])).astype(BF)
         wu[c, :, :, :, :, at] = g.reshape(wu.shape[1:5] + (256,))
 
 
@@ -259,21 +278,18 @@
     return jnp.concatenate(parts, axis=0)
 
 
-def qkv_backward(dqkv, na, wa, dnorm):
-    total, width = na.shape
+def qkv_normed(dqkv, wa, dnorm):
+    total = dqkv.shape[1]
 
     @pl.loop(0, 4)
     def _(i):
-        half = total // 4
-        rows = pl.ds(pl.multiple_of(i * half, half), half)
+        part = total // 4
+        rows = pl.ds(pl.multiple_of(i * part, part), part)
         dnorm[rows, :] = (
             nt(dqkv[0, rows, :], flat(wa[0]))
             + nt(dqkv[1, rows, :], flat(wa[1]))
             + nt(dqkv[2, rows, :], flat(wa[2]))
         )
-
-    for m in range(3):
-        wa[m] = grad_of(na, dqkv[m]).reshape(wa.shape[1:])
 
 
 def first_backward(picked, up, dnorm, dhid, gains, cols, new_grads, small, tile=128):
@@ -292,59 +308,6 @@
         d_first = r * (gains[0:1, :] * d - xr * mean)
         d_picked = d_first + dhid[rows, :] + cols[rows, DLOG : DLOG + 1] * gains[2:3, :]
         new_grads[rows, :] = (up[rows, :].astype(F32) + d_picked).astype(BF)
-
-
-def compute_kernel(
-    tokens, cot, idx, valid, wa_in, wu_in, wd_in, gains,
-    ga, gu, gd, small, new_rows, new_grads,
-    wa, wu, wd, picked, up, cols, na, qkv, probs, mixed, attn_out, nm, nmt, dd,
-    act, dup, down, dnm, tok_sem, w_sem,
-):
-    seqs, slots = idx.shape
-    width = picked.shape[1]
-    scale = (width // HEADS) ** -0.5
-    loads = [pltpu.make_async_copy(a, b, w_sem.at[i]) for i, (a, b) in enumerate(((wa_in, wa), (wu_in, wu), (wd_in, wd)))]
-    for l in loads:
-        l.start()
-    pick_phase(tokens, cot, idx, valid, picked, up, cols, (new_rows, new_grads), tok_sem)
-    norm_phase(picked, gains, cols, na)
-    loads[0].wait()
-    qkv_phase(na, wa, qkv, scale)
-
-    @pl.loop(0, seqs)
-    def _(s):
-        attention_forward(idx, valid, cols, qkv, probs, mixed, s)
-
-    out_phase(mixed, wa, attn_out)
-    mid_norm(picked, attn_out, up, gains, cols, nm, nmt, dd, down, dnm)
-    loads[1].wait()
-    loads[2].wait()
-    for c in range(wu.shape[0]):
-
-        @pl.loop(0, 4)
-        def _(n):
-            mlp_up(nm, dd, wu, wd, act, dup, c, n)
-
-        mlp_down(act, wd, down, c)
-        mlp_dnormed(dup, wu, dnm, c)
-        mlp_grad_down(act, dd, wd, c)
-        mlp_grad_up(nmt, dup, wu, c)
-    datt = nm
-    dmix = dd
-    mid_backward(picked, attn_out, up, down, dnm, gains, cols, datt, new_rows, small)
-    out_backward(datt, mixed, wa, dmix)
-
-    @pl.loop(0, seqs)
-    def _(s):
-        attention_backward(qkv, probs, mixed, dmix, s, slots, scale)
-
-    qkv_backward(qkv, na, wa, down)
-    first_backward(picked, up, down, dnm, gains, cols, new_grads, small)
-    outs = [pltpu.make_async_copy(a, b, w_sem.at[i]) for i, (a, b) in enumerate(((wa, ga), (wu, gu), (wd, gd)))]
-    for o in outs:
-        o.start()
-    for o in outs:
-        o.wait()
 
 
 MESH_ID = pl.DeviceIdType.MESH
@@ -710,94 +673,249 @@
         )
 
 
-def gather_kernel(depth, wq, wk, wv, wo, up, down, gpad, wa_out, wu_out, wd_out, gains_out,
-                  wa, wu, wd, gbox, own_sem, sends, recvs):
+def chunk_boxes(rows_a, width, rows_d, ff_c):
+    def boxes(n, rows, cols, first):
+        def box(*lead):
+            return pltpu.VMEM((n,) + lead + (rows, cols), BF)
+
+        return ([box(4, 2, 2)] if first else []) + [box(2, 2), box(2, 2), box(2), box(2), box(3)]
+
+    return (
+        boxes(CHUNKS, rows_a, ff_c // 2, True)
+        + boxes(CHUNKS, rows_d, width // 2, True)
+        + boxes(A_MATS, rows_a, width // 2, False)
+    )
+
+
+def block_kernel(
+    depth, tokens, cot, idx, valid, wq, wk, wv, wo, up_in, down_in, gpad,
+    new_rows, new_grads, fa, fu, fd, small_out,
+    wa, wu, wd, picked, up, cols, na, nmt, dd, qkv, probs, mixed, attn_out, act, dup, down, dnm,
+    gains, gbox, small, inbox,
+    tok_sem, own_sem, out_sem, ag_send, ag_recv, rs_send, rs_recv, frees, opened, *boxes,
+):
+    seqs, slots = idx.shape
+    width = picked.shape[1]
+    scale = (width // HEADS) ** -0.5
+    rows_a = wa.shape[-2]
+    half = width // 2
     me = Place(depth)
     me.greet()
-    own = Owned(me, (wq, wk, wv, wo, up, down), wa, wu, wd, own_sem)
-    ag = Gather(me, wa, wu, wd, sends, recvs)
-    arrays = range(7)
+    own = Owned(me, (wq, wk, wv, wo, up_in, down_in), wa, wu, wd, own_sem)
+    ag = Gather(me, wa, wu, wd, ag_send, ag_recv)
     gsem = 7 * Gather.SLOTS
-    def gcopy(o):
+    others = range(1, depth)
+
+    def gain_copy(o):
         return pltpu.make_async_remote_copy(
-            src_ref=gpad, dst_ref=gbox.at[o - 1], send_sem=sends.at[gsem + o], recv_sem=recvs.at[gsem + o],
-            device_id=me.at_z(me.ahead(o)), device_id_type=MESH_ID)
-    for o in range(1, depth):
-        gcopy(o).start()
-    for a in arrays:
+            src_ref=gpad, dst_ref=gbox.at[o - 1], send_sem=ag_send.at[gsem + o], recv_sem=ag_recv.at[gsem + o],
+            device_id=me.at_z(me.ahead(o)), device_id_type=MESH_ID,
+        )
+
+    def spread(*arrays):
+        for a in arrays:
+            for o in others:
+                ag.spread(a, o)
+
+    def forward(*arrays):
+        for a in arrays:
+            for o in others:
+                ag.forward(a, o)
+
+    def across(*arrays):
+        for a in arrays:
+            ag.across(a)
+
+    own.start(0)
+    picker = Picker(tokens, cot, picked, up, cols, (act, dup), tok_sem)
+    for a in range(1, 7):
         own.start(a)
-    for a in arrays:
+    picker.start(0)
+    own.wait(0)
+    ag.send_z(0)
+    for o in others:
+        gain_copy(o).start()
+    for a in range(1, 7):
         own.wait(a)
         ag.send_z(a)
-    for t in range(len(arrays) + 3):
-        if t < 7:
-            for o in range(1, depth):
-                ag.spread(t, o)
-        if 0 <= t - 1 < 7:
-            for o in range(1, depth):
-                ag.forward(t - 1, o)
-        if 0 <= t - 2 < 7:
-            ag.across(t - 2)
-        if 0 <= t - 3 < 7:
-            ag.ready(t - 3)
+    picker.turn(idx, valid)
+    picker.pick(0, slots, True)
+    picker.pick(1, slots, True)
+    spread(0)
+    picker.pick(2, slots, True)
+    picker.pick(3, slots, False)
     total = gpad[...].astype(F32)
-    for o in range(1, depth):
-        gcopy(o).wait()
+    for o in others:
+        gain_copy(o).wait()
         total = total + gbox[o - 1].astype(F32)
-    gains_out[...] = total[:8]
-    for a in arrays:
-        ag.settle(a)
-    outs = [pltpu.make_async_copy(a, b, own_sem.at[i]) for i, (a, b) in enumerate(((wa, wa_out), (wu, wu_out), (wd, wd_out)))]
-    for o in outs:
-        o.start()
-    for o in outs:
-        o.wait()
-
-
-def reduce_scratch(total_depth, rows_a, width, rows_d, ff_c):
-    def boxes(n, rows, cols):
-        v = lambda *s: pltpu.VMEM((n,) + s + (rows, cols), BF)
-        return [v(4, 2, 2), v(2, 2), v(2, 2), v(2), v(2), v(3)]
-    return boxes(4, rows_a, width // 2) + boxes(3, rows_a, ff_c // 2) + boxes(3, rows_d, width // 2)
-
-
-def reducers(me, wa, wu, wd, boxes, sends, recvs, frees):
-    out = []
-    for w, b, ways in ((wa, boxes[0:6], (0, 1, 0, 1)), (wu, boxes[6:12], (0, 0, 0)), (wd, boxes[12:18], (1, 1, 1))):
-        for i, way in enumerate(ways):
-            out.append(Reduce(me, w.at[i], *[x.at[i] for x in b], sends, recvs, frees, len(out), way))
-    return out
-
-
-def reduce_kernel(depth, ga, gu, gd, small_in, fa, fu, fd, small_out,
-                  wa, wu, wd, small, inbox, load_sem, sends, recvs, frees, *boxes):
-    me = Place(depth)
-    me.greet()
-    loads = [pltpu.make_async_copy(a, b, load_sem.at[i]) for i, (a, b) in enumerate(((ga, wa), (gu, wu), (gd, wd)))]
-    for l in loads:
-        l.start()
-    for l in loads:
-        l.wait()
-    rs = reducers(me, wa, wu, wd, boxes, sends, recvs, frees)
-    order = [4, 7, 5, 8, 6, 9, 3, 0, 1, 2]
-    ss = SmallSum(me, small, inbox, sends, recvs, 10 * Reduce.SLOTS)
-    small[0] = small_in[...]
-    steps = ("t1", "t2", "t3", "t4", "t5", "t6", "t7", "t8")
-    for t in range(len(order) + len(steps) - 1):
-        for k in range(len(steps)):
-            if 0 <= t - k < len(order):
-                getattr(rs[order[t - k]], steps[k])()
-    for k in range(5):
-        ss.step(k)
+    gains[...] = total[:8]
+    norm_phase(picked, gains, cols, na)
+    forward(0)
+    spread(1, 2)
+    across(0)
+    ag.ready(0)
+    qkv_phase(na, wa, qkv, scale)
+    spread(3, 4)
+    forward(1, 2)
+
+    @pl.loop(0, seqs)
+    def _(s):
+        attention_forward(idx, valid, cols, qkv, probs, mixed, s)
+
+        @pl.when(s == 0)
+        def _():
+            across(1, 2)
+            spread(5, 6)
+            forward(3, 4)
+
+        @pl.when(s == 1)
+        def _():
+            across(3, 4)
+            forward(5, 6)
+
+        @pl.when(s == 2)
+        def _():
+            across(5, 6)
+
+    out_phase(mixed, wa, attn_out)
+    mid_norm(picked, attn_out, up, gains, cols, na, nmt, dd)
+
+    ubox, dbox, abox = boxes[0:6], boxes[6:12], boxes[12:17]
+    reducers = {}
+
+    def reducer(name, at, w, core_box, rest, i, way):
+        reducers[name] = Reduce(me, w, core_box, *[x.at[i] for x in rest], rs_send, rs_recv, frees, at, way)
+
+    for c in range(CHUNKS):
+        reducer("u%d" % c, c, wu.at[c], ubox[0].at[c], ubox[1:], c, 0)
+        reducer("d%d" % c, 3 + c, wd.at[c], dbox[0].at[c], dbox[1:], c, 1)
+    spots = ((act, 0), (act, half), (dup, 0), (dup, half))
+    terms = [probs.at[m, :, :, :, 0:rows_a, 0:width] for m in range(3)] + [wa.at[3]]
+    for m, name in enumerate("qkvo"):
+        ref, lane = spots[m]
+        box = ref.at[:, :, :, 0:rows_a, lane : lane + half]
+        reducer(name, 6 + m, terms[m], box, abox, m, m % 2)
+    finals = {"q": (fa, 0), "k": (fa, 1), "v": (fa, 2), "o": (fa, 3)}
+    for c in range(CHUNKS):
+        finals["u%d" % c] = (fu, c)
+        finals["d%d" % c] = (fd, c)
+    order = list(finals)
+
+    def result_copies(name):
+        dst, i = finals[name]
+        box = reducers[name].from_core
+        base = 2 * order.index(name)
+        for h, core in ((0, me.core), (1, 1 - me.core)):
+            yield pltpu.make_async_copy(box.at[h], dst.at[i, :, :, :, half_of(dst, core)], out_sem.at[base + h])
+
+    def step(k, *names):
+        for name in names:
+            getattr(reducers[name], "t%d" % k)()
+            if k == 8:
+                for c in result_copies(name):
+                    c.start()
+
+    for c in range(CHUNKS):
+        for a in (1 + 2 * c, 2 + 2 * c):
+            ag.ready(a)
+
+        @pl.loop(0, 4)
+        def _(n):
+            mlp_up(na, dd, wu, wd, act, dup, c, n)
+
+        if c == 1:
+            step(2, "u0", "d0")
+        if c == 2:
+            step(4, "u0", "d0")
+            step(2, "u1", "d1")
+        mlp_down(act, wd, down, c)
+        mlp_dnormed(dup, wu, dnm, c)
+        if c == 2:
+            step(5, "u0", "d0")
+        ag.settle(1 + 2 * c)
+        ag.settle(2 + 2 * c)
+        mlp_grad_down(act, dd, wd, c)
+        step(1, "d%d" % c)
+        mlp_grad_up(nmt, dup, wu, c)
+        step(1, "u%d" % c)
+        if c == 1:
+            step(3, "u0", "d0")
+        if c == 2:
+            step(3, "u1", "d1")
+            step(6, "u0", "d0")
+    pl.semaphore_signal(opened, inc=1, device_id=me.sib, device_id_type=MESH_ID)
+    ag.settle(0)
+    datt, dmix = na, dd
+    mid_backward(picked, attn_out, up, down, dnm, gains, cols, datt, dd, small.at[0])
+    rows_out = pltpu.make_async_copy(dd, new_rows, tok_sem.at[0])
+    rows_out.start()
+    step(2, "u2", "d2")
+    step(4, "u1", "d1")
+    step(7, "u0", "d0")
+    rows_out.wait()
+    out_backward(datt, mixed, wa, dmix)
+    pl.semaphore_wait(opened, 1)
+    step(1, "o")
+    step(8, "u0", "d0")
+    norm_again(picked, gains, cols, na)
+
+    @pl.loop(0, seqs)
+    def _(s):
+        attention_backward(qkv, probs, mixed, dmix, s, slots, scale)
+
+        @pl.when(s == 0)
+        def _():
+            step(3, "u2", "d2")
+            step(5, "u1", "d1")
+            step(2, "o")
+
+        @pl.when(s == 1)
+        def _():
+            step(4, "u2", "d2")
+            step(6, "u1", "d1")
+            step(3, "o")
+
+        @pl.when(s == 2)
+        def _():
+            step(5, "u2", "d2")
+            step(7, "u1", "d1")
+            step(4, "o")
+
+    for m, name in enumerate("qkv"):
+        terms[m][...] = grad_of(na, qkv[m]).reshape(wa.shape[1:])
+        step(1, name)
+        if m > 0:
+            step(2, "qkv"[m - 1])
+    step(6, "u2", "d2")
+    step(8, "u1", "d1")
+    step(5, "o")
+    qkv_normed(qkv, wa, down)
+    step(2, "v")
+    first_backward(picked, up, down, dnm, gains, cols, dd, small.at[0])
+    grads_out = pltpu.make_async_copy(dd, new_grads, tok_sem.at[1])
+    grads_out.start()
+    sums = SmallSum(me, small, inbox, rs_send, rs_recv, 10 * Reduce.SLOTS)
+    sums.step(0)
+    step(3, *"qkv")
+    step(7, "u2", "d2")
+    step(6, "o")
+    sums.step(1)
+    step(4, *"qkv")
+    sums.step(2)
+    step(8, "u2", "d2")
+    step(7, "o")
+    sums.step(3)
+    step(5, *"qkv")
+    step(8, "o")
+    step(6, *"qkv")
+    sums.step(4)
+    step(7, *"qkv")
+    step(8, *"qkv")
     small_out[...] = small[4]
-    outs = []
-    for box, dst in ((boxes[0], fa), (boxes[6], fu), (boxes[12], fd)):
-        for h, core in ((0, me.core), (1, 1 - me.core)):
-            outs.append(pltpu.make_async_copy(box.at[:, h], dst.at[:, :, :, :, half_of(dst, core)], load_sem.at[len(outs)]))
-    for o in outs:
-        o.start()
-    for o in outs:
-        o.wait()
+    for name in order:
+        for c in result_copies(name):
+            c.wait()
+    grads_out.wait()
 
 
 def place_kernel(idx, tokens, cot, new_rows, new_grads, fa, fu, fd,
@@ -857,36 +975,32 @@
     gpad = lax.dynamic_update_slice(jnp.zeros((16, width), BF), gains3, (0, z * own))
     squares = [w.reshape(2, 2, rq, width) for w in (w_query, w_key, w_value, w_out)]
     sa, su, sdn = (A_MATS, depth, 2, 2, rq, width), (CHUNKS, depth, 2, 2, rq, cw), (CHUNKS, depth, 2, 2, dq, width)
-    nag = 7 * Gather.SLOTS + 8
-    wa, wu, wd, gains = pl.pallas_call(
-        functools.partial(gather_kernel, depth),
-        out_shape=(sd(sa, BF), sd(su, BF), sd(sdn, BF), sd((8, width), F32)),
-        in_specs=[hbm] * 6 + [vm], out_specs=(hbm, hbm, hbm, vm),
-        scratch_shapes=[vmem(sa, BF), vmem(su, BF), vmem(sdn, BF), vmem((depth - 1, 16, width), BF), sem((16,)), sem((nag,)), sem((nag,))],
-        compiler_params=remote_params(0),
-    )(*squares, w_up.reshape(2, 2, rq, ff), w_down.reshape(CHUNKS, 2, 2, dq, width), gpad)
+    nag, nrs = 7 * Gather.SLOTS + 8, 10 * Reduce.SLOTS + 8
     rows = (total, width)
-    ga, gu, gd, small, new_rows, new_grads = pl.pallas_call(
-        compute_kernel,
-        out_shape=(sd(sa, BF), sd(su, BF), sd(sdn, BF), sd((8, width), F32), sd(rows, BF), sd(rows, BF)),
-        in_specs=[hbm, hbm, vm, vm, hbm, hbm, hbm, vm], out_specs=(hbm, hbm, hbm, vm, vm, vm),
+    work = (4, 2, 2, total // 16, cw)
+    regular = pltpu.SemaphoreType.REGULAR
+    blocks = (seqs, 4, 2, 2, length // 16, width)
+    new_rows, new_grads, fa, fu, fd, sums = pl.pallas_call(
+        functools.partial(block_kernel, depth),
+        out_shape=(
+            sd(rows, BF), sd(rows, BF), sd(sa[:1] + sa[2:], BF), sd(su[:1] + su[2:], BF), sd(sdn[:1] + sdn[2:], BF),
+            sd((8, width), F32),
+        ),
+        in_specs=[hbm, hbm, vm, vm] + [hbm] * 6 + [vm],
+        out_specs=(hbm,) * 5 + (vm,),
         scratch_shapes=[
             vmem(sa, BF), vmem(su, BF), vmem(sdn, BF), vmem(rows, BF), vmem(rows, BF), vmem((total, 128), F32),
-            vmem(rows, BF), vmem((3,) + rows, BF), vmem((seqs * width // 128, 2 * slots, slots), BF), vmem(rows, BF),
-            vmem(rows, F32), vmem(rows, BF), vmem((width, total), BF), vmem(rows, BF), vmem((total, cw), BF),
-            vmem((total, cw), BF), vmem(rows, F32), vmem(rows, F32), sem((2,)), sem((3,)),
-        ],
-        compiler_params=pltpu.CompilerParams(vmem_limit_bytes=60 * 2**20),
-    )(tokens, cotangent, row_index, row_valid, wa, wu, wd, gains)
-    nrs = 10 * Reduce.SLOTS + 8
-    fa, fu, fd, sums = pl.pallas_call(
-        functools.partial(reduce_kernel, depth),
-        out_shape=(sd(sa[:1] + sa[2:], BF), sd(su[:1] + su[2:], BF), sd(sdn[:1] + sdn[2:], BF), sd((8, width), F32)),
-        in_specs=[hbm, hbm, hbm, vm], out_specs=(hbm, hbm, hbm, vm),
-        scratch_shapes=[vmem(sa, BF), vmem(su, BF), vmem(sdn, BF), vmem((5, 8, width), F32), vmem((2 + depth, 8, width), F32),
-                        sem((6,)), sem((nrs,)), sem((nrs,)), pltpu.SemaphoreType.REGULAR((10,))] + reduce_scratch(depth, rq, width, dq, cw),
-        compiler_params=remote_params(1),
-    )(ga, gu, gd, small)
+            vmem(rows, BF), vmem((width, total), BF), vmem(rows, BF), vmem((3,) + rows, BF), vmem((3,) + work, BF),
+            vmem(rows, BF), vmem(rows, F32), vmem(work, BF), vmem(work, BF), vmem(rows, F32), vmem(rows, F32),
+            vmem((8, width), F32), vmem((depth - 1, 16, width), BF), vmem((5, 8, width), F32), vmem((2 + depth, 8, width), F32),
+            sem((2,)), sem((16,)), sem((20,)), sem((nag,)), sem((nag,)), sem((nrs,)), sem((nrs,)), regular((10,)), regular,
+        ]
+        + chunk_boxes(rq, width, dq, cw),
+        compiler_params=remote_params(0, 63),
+    )(
+        tokens.reshape(blocks), cotangent.reshape(blocks), row_index, row_valid, *squares,
+        w_up.reshape(2, 2, rq, ff), w_down.reshape(CHUNKS, 2, 2, dq, width), gpad,
+    )
     fa, fu, fd, sums = over_groups(groups, (fa, fu, fd, sums))
     out, grad, gq, gk, gv, go, gup, gdown = pl.pallas_call(
         place_kernel,

time: 319 us -> 231 us (0.72)
  Pallas kernels: 309 us -> 221 us
    pallas_call x3 -> x1, Pallas kernels: 296 us -> 208 us  [body(): pl.pallas_call(functools.partial(block_kernel, depth), out_shape=(sd(rows...]
where the time goes in v2:
time: 231 us; the launch traced here: 230 us
  Pallas kernels  221 us (96%)
  local copies, waits for them, and re-layouts  8.34 us (4%)
    pallas_call x1, Pallas kernels, body(): pl.pallas_call(functools.partial(block_kernel, depth), out_shape=(sd(rows...  208 us
    pallas_call x1, Pallas kernels, body(): pl.pallas_call(place_kernel, grid=(seqs,), out_shape=(sd(tokens.shape, BF...  12.9 us

profile of v2, /device:TPU:0, one launch (start us, length us, event | category | flops | bytes accessed | tf_op | source)
XLA Modules:
  0.0 230.3 jit_solution(261010295738103338)
XLA Ops:
  0.6 0.7 stack.12
  1.3 0.7 stack.13
  2.0 0.7 stack.14
  2.6 0.5 dynamic_update_slice.3.gpad
  3.1 0.0 copy-start.4
  3.1 0.6 copy-done.4
  3.7 0.0 copy-start.3
  3.7 208.2 %shard_map.212 = (bf16[1024,768]{1,0:T(8,128)(2,1)}, bf16[1024,768]{1,0:T(8,128)(2,1)}, bf16[4,2,2,48,768]{4,3,2,1,0:T(8,128)(2,1)}, bf16[3,2,2,48,1024]{4,3,2,1...) custom-call(bf16[4,4,2,2,64,768]{5,4,3,2,1,0:T(8,128)(2,1)} %bitcast.18, ...), custom_call_target="tpu_custom_call" | custom-call | tf_op jit(solution)/shard_map/pallas_call | solution.py:983
  211.9 1.5 fusion
  213.4 0.0 copy-done.3
  213.4 0.0 copy-start
  213.4 1.3 copy-done
  214.7 0.0 copy-start.1
  214.7 1.3 copy-done.1
  216.0 0.0 copy-start.2
  216.0 1.3 copy-done.2
  217.2 12.9 %shard_map.213 = (bf16[4096,768]{1,0:T(8,128)(2,1)}, bf16[4096,768]{1,0:T(8,128)(2,1)}, f32[192,768]{1,0:T(8,128)}, f32[192,768]{1,0:T(8,128)}, f32[192,768]{1,0...) custom-call(s32[4,256]{1,0:T(4,128)S(1)} %copy-done.3, bf16[4096,768]{1,0:T(8,128)(2,1)} %tokens.1, ...), custom_call_target="tpu_custom_call" | custom-call | tf_op jit(solution)/shard_map/pallas_call | solution.py:1005
  (2 shorter events, 0.0 us)
Async XLA Ops:
  3.1 0.6 copy-start.4
  3.7 209.7 %copy-start.3 = (s32[4,256]{1,0:T(4,128)S(1)}, s32[4,256]{1,0:T(4,128)}, u32[]{:S(2)}) copy-start(s32[4,256]{1,0:T(4,128)} %idx.3) | copy-start | bytes 12292
  213.4 1.3 copy-start
  214.7 1.3 copy-start.1
  216.0 1.3 copy-start.2

commit v3 on v2

--- a/solution.py
+++ b/solution.py
@@ -91,17 +91,14 @@
         na[rows, :] = (x * cols[rows, R1 : R1 + 1] * gains[0:1, :]).astype(BF)
 
 
-def qkv_phase(na, wa, qkv, scale):
-    width = na.shape[1]
-    for m in range(3):
-
-        @pl.loop(0, width // 256)
-        def _(n):
-            at = pl.ds(pl.multiple_of(n * 256, 256), 256)
-            out = nn(na[...], flat(wa[m, :, :, :, :, at]))
-            if m == 0:
-                out = out * scale
-            qkv[m, :, at] = out.astype(BF)
+def qkv_one(na, wa, qkv, scale, m):
+    @pl.loop(0, na.shape[1] // 256)
+    def _(n):
+        at = pl.ds(pl.multiple_of(n * 256, 256), 256)
+        out = nn(na[...], flat(wa[m, :, :, :, :, at]))
+        if m == 0:
+            out = out * scale
+        qkv[m, :, at] = out.astype(BF)
 
 
 def two_heads(v2, low_half):
@@ -351,126 +348,89 @@
 
 
 class Gather:
-    SLOTS = 18
+    SENDS, RECVS = 2, 5
+    CORE, Z, X, Y, FAR = range(5)
+    ARRAYS = A_MATS + 2 * CHUNKS
 
     def __init__(self, me, wa, wu, wd, sends, recvs):
         self.me, self.refs, self.sends, self.recvs = me, (wa, wu, wd), sends, recvs
 
+    def array(self, a):
+        wa, wu, wd = self.refs
+        if a < A_MATS:
+            return wa.at[a]
+        return (wd if a % 2 else wu).at[(a - A_MATS) // 2]
+
     def piece(self, a, zi, xi, yi, core):
-        wa, wu, wd = self.refs
-        if a == 0:
-            return wa.at[:, zi, xi, yi, :, half_of(wa, core)]
-        ref = wu if a % 2 else wd
-        return ref.at[(a - 1) // 2, zi, xi, yi, :, half_of(ref, core)]
-
-    def part(self, a, zi, xi, yi, core, h):
-        wa = self.refs[0]
-        if a == 0:
-            return wa.at[2 * h : 2 * h + 2, zi, xi, yi, :, half_of(wa, core)]
-        return self.piece(a, zi, xi, yi, core)
-
-    def ways(self, a):
-        return (0, 1) if a == 0 else ((0,) if a % 2 else (1,))
-
-    def copy(self, a, k, ref, dev):
-        at = a * self.SLOTS + k
+        ref = self.array(a)
+        return ref.at[zi, xi, yi, :, half_of(ref, core)]
+
+    def way(self, a):
+        return a % 2
+
+    def copy(self, a, kind, ref, dev):
+        send = self.sends.at[a * self.SENDS + (0 if kind == self.CORE else 1)]
+        recv = self.recvs.at[a * self.RECVS + kind]
         return pltpu.make_async_remote_copy(
-            src_ref=ref, dst_ref=ref, send_sem=self.sends.at[at], recv_sem=self.recvs.at[at],
-            device_id=dev, device_id_type=MESH_ID,
+            src_ref=ref, dst_ref=ref, send_sem=send, recv_sem=recv, device_id=dev, device_id_type=MESH_ID
         )
 
-    def z_out(self, a, o):
+    def mine(self, a, zi, flip_x=False, flip_y=False):
         m = self.me
-        return self.copy(a, o, self.piece(a, m.z, m.x, m.y, m.core), m.at_z(m.ahead(o)))
-
-    def x_out(self, a, o):
-        m = self.me
-        return self.copy(a, 3 + o, self.piece(a, m.behind(o), m.x, m.y, m.core), m.xn)
-
-    def y_out(self, a, o):
-        m = self.me
-        return self.copy(a, 6 + o, self.piece(a, m.behind(o), m.x, m.y, m.core), m.yn)
-
-    def far_out(self, a, o, h):
-        m = self.me
-        if h == 0:
-            return self.copy(a, 9 + o, self.part(a, m.behind(o), 1 - m.x, m.y, m.core, 0), m.yn)
-        return self.copy(a, 12 + o, self.part(a, m.behind(o), m.x, 1 - m.y, m.core, 1), m.xn)
-
-    def core_out(self, a):
-        m = self.me
-        wa, wu, wd = self.refs
-        if a == 0:
-            ref = wa.at[:, :, :, :, :, half_of(wa, m.core)]
-        else:
-            ref = wu if a % 2 else wd
-            ref = ref.at[(a - 1) // 2, :, :, :, :, half_of(ref, m.core)]
-        return self.copy(a, 0, ref, m.sib)
-
-    def z_in(self, a, o):
-        m = self.me
-        return self.copy(a, o, self.piece(a, m.behind(o), m.x, m.y, m.core), m.at_z(m.behind(o)))
-
-    def x_in(self, a, o):
-        m = self.me
-        return self.copy(a, 3 + o, self.piece(a, m.behind(o), 1 - m.x, m.y, m.core), m.xn)
-
-    def y_in(self, a, o):
-        m = self.me
-        return self.copy(a, 6 + o, self.piece(a, m.behind(o), m.x, 1 - m.y, m.core), m.yn)
-
-    def far_in(self, a, o, h):
-        m = self.me
-        part = self.part(a, m.behind(o), 1 - m.x, 1 - m.y, m.core, h)
-        return self.copy(a, (9 if h == 0 else 12) + o, part, m.yn if h == 0 else m.xn)
-
-    def core_in(self, a):
-        m = self.me
-        wa, wu, wd = self.refs
-        if a == 0:
-            ref = wa.at[:, :, :, :, :, half_of(wa, 1 - m.core)]
-        else:
-            ref = wu if a % 2 else wd
-            ref = ref.at[(a - 1) // 2, :, :, :, :, half_of(ref, 1 - m.core)]
-        return self.copy(a, 0, ref, m.sib)
+        return self.piece(a, zi, 1 - m.x if flip_x else m.x, 1 - m.y if flip_y else m.y, m.core)
+
+    def took(self, a, kind):
+        self.copy(a, kind, self.mine(a, slice(0, self.me.depth - 1)), self.me.xn).wait_recv()
+
+    def core_copy(self, a, core):
+        ref = self.array(a)
+        return self.copy(a, self.CORE, ref.at[:, :, :, :, half_of(ref, core)], self.me.sib)
 
     def origins(self):
         return range(1, self.me.depth)
 
     def send_z(self, a):
+        m = self.me
         for o in self.origins():
-            self.z_out(a, o).start()
-
-    def spread(self, a, o):
-        self.z_in(a, o).wait_recv()
-        self.x_out(a, o).start()
-        self.y_out(a, o).start()
-
-    def forward(self, a, o):
-        self.x_in(a, o).wait_recv()
-        if 0 in self.ways(a):
-            self.far_out(a, o, 0).start()
-        self.y_in(a, o).wait_recv()
-        if 1 in self.ways(a):
-            self.far_out(a, o, 1).start()
+            self.copy(a, self.Z, self.mine(a, m.z), m.at_z(m.ahead(o))).start()
+
+    def spread(self, a):
+        m = self.me
+        self.took(a, self.Z)
+        for o in self.origins():
+            self.copy(a, self.X, self.mine(a, m.behind(o)), m.xn).start()
+            self.copy(a, self.Y, self.mine(a, m.behind(o)), m.yn).start()
+
+    def forward(self, a):
+        m, by_x = self.me, self.way(a) == 0
+        self.took(a, self.X if by_x else self.Y)
+        for o in self.origins():
+            ref = self.mine(a, m.behind(o), by_x, not by_x)
+            self.copy(a, self.FAR, ref, m.yn if by_x else m.xn).start()
 
     def across(self, a):
-        for o in self.origins():
-            for h in self.ways(a):
-                self.far_in(a, o, h).wait_recv()
-        self.core_out(a).start()
+        self.took(a, self.Y if self.way(a) == 0 else self.X)
+        self.took(a, self.FAR)
+        self.core_copy(a, self.me.core).start()
 
     def ready(self, a):
-        self.core_in(a).wait_recv()
+        self.core_copy(a, 1 - self.me.core).wait_recv()
 
     def settle(self, a):
-        for o in self.origins():
-            self.z_out(a, o).wait_send()
-            self.x_out(a, o).wait_send()
-            self.y_out(a, o).wait_send()
-            for h in self.ways(a):
-                self.far_out(a, o, h).wait_send()
-        self.core_out(a).wait_send()
+        m, ref = self.me, self.array(a)
+        self.core_copy(a, m.core).wait_send()
+        sent = ref.at[0 : m.depth - 1, :, :, :, half_of(ref, m.core)]
+        self.copy(a, self.Z, sent, m.xn).wait_send()
+
+    def slot(self, t, ahead=2):
+        if t < self.ARRAYS:
+            self.spread(t)
+        if ahead <= t + ahead < self.ARRAYS:
+            self.send_z(t + ahead)
+        if 0 <= t - 1 < self.ARRAYS:
+            self.forward(t - 1)
+        if 0 <= t - 2 < self.ARRAYS:
+            self.across(t - 2)
 
 
 class Owned:
@@ -478,23 +438,22 @@
         wq, wk, wv, wo, up, down = shards
         z, core = me.z, me.core
         half = half_of(wa, core)
-        self.copies = {0: [], 1: [], 2: [], 3: [], 4: [], 5: [], 6: []}
+        self.copies = {a: [] for a in range(Gather.ARRAYS)}
         for m, w in enumerate((wq, wk, wv, wo)):
-            self.copies[0].append((w.at[:, :, :, half], wa.at[m, z, :, :, :, half]))
+            self.copies[m].append((w.at[:, :, :, half], wa.at[m, z, :, :, :, half]))
         ff_own = up.shape[-1] // me.depth
         for c in range(CHUNKS):
             for j in range(2):
                 block = 2 * core + j
                 src = up.at[:, :, :, pl.ds(pl.multiple_of(block * ff_own + c * 256, 128), 256)]
                 dst = wu.at[c, z, :, :, :, pl.ds(pl.multiple_of(block * 256, 128), 256)]
-                self.copies[1 + 2 * c].append((src, dst))
-            self.copies[2 + 2 * c].append((down.at[c, :, :, :, half], wd.at[c, z, :, :, :, half]))
+                self.copies[A_MATS + 2 * c].append((src, dst))
+            self.copies[A_MATS + 1 + 2 * c].append((down.at[c, :, :, :, half], wd.at[c, z, :, :, :, half]))
         self.sems = sems
 
     def all_of(self, a):
-        base = sum(len(self.copies[b]) for b in range(a))
         for i, (src, dst) in enumerate(self.copies[a]):
-            yield pltpu.make_async_copy(src, dst, self.sems.at[base + i])
+            yield pltpu.make_async_copy(src, dst, self.sems.at[2 * a + i])
 
     def start(self, a):
         for c in self.all_of(a):
@@ -506,62 +465,50 @@
 
 
 class Reduce:
-    SLOTS = 14
+    SENDS, RECVS = 2, 7
+    CORE, FIRST, SECOND, Z, BACK, FAR, LAST = range(7)
 
     def __init__(
         self, me, w, from_core, from_x, from_y, then_x, then_y, from_z, sends, recvs, frees, at, way
     ):
-        self.me, self.w, self.way, self.free, base = me, w, way, frees.at[at], at * self.SLOTS
+        self.me, self.w, self.way, self.free, base = me, w, way, frees.at[at], at
         self.from_core, self.from_x, self.from_y = from_core, from_x, from_y
         self.then_x, self.then_y, self.from_z = then_x, then_y, from_z
         self.sends, self.recvs, self.base = sends, recvs, base
         self.mine, self.theirs = half_of(w, me.core), half_of(w, 1 - me.core)
 
-    def copy(self, k, src, dst, dev):
-        at = self.base + k
+    def copy(self, kind, src, dst, dev):
+        small = kind in (self.Z, self.BACK, self.FAR)
+        send = self.sends.at[self.base * self.SENDS + small]
+        recv = self.recvs.at[self.base * self.RECVS + kind]
         return pltpu.make_async_remote_copy(
-            src_ref=src, dst_ref=dst, send_sem=self.sends.at[at], recv_sem=self.recvs.at[at],
-            device_id=dev, device_id_type=MESH_ID,
+            src_ref=src, dst_ref=dst, send_sem=send, recv_sem=recv, device_id=dev, device_id_type=MESH_ID
         )
 
-    def core_copy(self):
-        return self.copy(0, self.w.at[:, :, :, :, self.theirs], self.from_core, self.me.sib)
-
-    def plane_first(self):
-        m, w = self.me, self.w
-        return (
-            self.copy(1, w.at[0:2, 1 - m.x, :, :, self.mine], self.from_x, m.xn),
-            self.copy(2, w.at[2:4, :, 1 - m.y, :, self.mine], self.from_y, m.yn),
-        )
-
-    def plane_second(self):
-        m, w = self.me, self.w
-        return (
-            self.copy(3, w.at[0:2, m.x, 1 - m.y, :, self.mine], self.then_y, m.yn),
-            self.copy(4, w.at[2:4, 1 - m.x, m.y, :, self.mine], self.then_x, m.xn),
-        )
+    def took(self, kind, ref):
+        self.copy(kind, ref, ref, self.me.sib).wait_recv()
+
+    def sent(self, kind, ref):
+        self.copy(kind, ref, ref, self.me.sib).wait_send()
 
     def z_copy(self, o):
         m = self.me
         src = self.w.at[m.ahead(o), m.x, m.y, :, self.mine]
-        return self.copy(4 + o, src, self.from_z.at[o - 1], m.at_z(m.ahead(o)))
-
-    def back(self, k, xi, yi, dev):
+        return self.copy(self.Z, src, self.from_z.at[o - 1], m.at_z(m.ahead(o)))
+
+    def back(self, kind, xi, yi, dev):
         ref = self.from_core.at[0, xi, yi]
-        return self.copy(k, ref, ref, dev)
-
-    def core_back(self):
-        return self.copy(11, self.from_core.at[0], self.from_core.at[1], self.me.sib)
+        return self.copy(kind, ref, ref, dev)
 
     def add(self, at, arrived):
         self.w[at] = (self.w[at].astype(F32) + arrived.astype(F32)).astype(BF)
 
     def t1(self):
-        self.core_copy().start()
+        self.copy(self.CORE, self.w.at[:, :, :, :, self.theirs], self.from_core, self.me.sib).start()
 
     def t2(self):
-        m = self.me
-        self.core_copy().wait()
+        m, w = self.me, self.w
+        self.took(self.CORE, self.from_core)
 
         @pl.loop(0, 2 * m.depth)
         def _(i):
@@ -569,66 +516,58 @@
             self.add((zi, xi, slice(None), slice(None), self.mine), self.from_core[zi, xi])
 
         pl.semaphore_signal(self.free, inc=1, device_id=m.sib, device_id_type=MESH_ID)
-        for c in self.plane_first():
-            c.start()
+        self.copy(self.FIRST, w.at[0:2, 1 - m.x, :, :, self.mine], self.from_x, m.xn).start()
+        self.copy(self.FIRST, w.at[2:4, :, 1 - m.y, :, self.mine], self.from_y, m.yn).start()
 
     def t3(self):
-        m = self.me
-        first = self.plane_first()
-        first[0].wait()
-        for zi in range(2):
+        m, w = self.me, self.w
+        self.took(self.FIRST, w.at[0:2, :, :, :, self.mine])
+
+        @pl.loop(0, 2)
+        def _(zi):
             self.add((zi, m.x, slice(None), slice(None), self.mine), self.from_x[zi])
-        first[1].wait()
-        for zi in range(2):
             self.add((2 + zi, slice(None), m.y, slice(None), self.mine), self.from_y[zi])
-        for c in self.plane_second():
-            c.start()
+
+        self.copy(self.SECOND, w.at[0:2, m.x, 1 - m.y, :, self.mine], self.then_y, m.yn).start()
+        self.copy(self.SECOND, w.at[2:4, 1 - m.x, m.y, :, self.mine], self.then_x, m.xn).start()
 
     def t4(self):
         m = self.me
-        second = self.plane_second()
-        second[0].wait()
+        self.took(self.SECOND, self.w.at[0:2, 0:2, 0, :, self.mine])
         self.add((slice(0, 2), m.x, m.y, slice(None), self.mine), self.then_y[...])
-        second[1].wait()
         self.add((slice(2, 4), m.x, m.y, slice(None), self.mine), self.then_x[...])
         for o in range(1, m.depth):
             self.z_copy(o).start()
 
     def t5(self):
         m = self.me
-        at = (m.z, m.x, m.y, slice(None), self.mine)
-        total = self.w[at].astype(F32)
+        total = self.w[m.z, m.x, m.y, :, self.mine].astype(F32)
+        self.took(self.Z, self.from_z)
         for o in range(1, m.depth):
-            self.z_copy(o).wait()
             total = total + self.from_z[o - 1].astype(F32)
         self.from_core[0, m.x, m.y] = total.astype(BF)
-        self.back(8, m.x, m.y, m.xn).start()
-        self.back(9, m.x, m.y, m.yn).start()
-
-    def far(self):
-        m = self.me
-        if self.way == 0:
-            return self.back(10, 1 - m.x, m.y, m.yn)
-        return self.back(10, m.x, 1 - m.y, m.xn)
+        self.back(self.BACK, m.x, m.y, m.xn).start()
+        self.back(self.BACK, m.x, m.y, m.yn).start()
 
     def t6(self):
         m = self.me
-        self.back(8, 1 - m.x, m.y, m.xn).wait_recv()
-        self.back(9, m.x, 1 - m.y, m.yn).wait_recv()
-        self.far().start()
+        self.took(self.BACK, self.from_core.at[0, 0:2, 0])
+        if self.way == 0:
+            self.back(self.FAR, 1 - m.x, m.y, m.yn).start()
+        else:
+            self.back(self.FAR, m.x, 1 - m.y, m.xn).start()
 
     def t7(self):
         m = self.me
-        self.back(10, 1 - m.x, 1 - m.y, m.yn if self.way == 0 else m.xn).wait_recv()
+        self.took(self.FAR, self.from_core.at[0, 0, 0])
         pl.semaphore_wait(self.free, 1)
-        self.core_back().start()
+        self.copy(self.LAST, self.from_core.at[0], self.from_core.at[1], m.sib).start()
 
     def t8(self):
         m = self.me
-        self.core_back().wait()
-        self.back(8, m.x, m.y, m.xn).wait_send()
-        self.back(9, m.x, m.y, m.yn).wait_send()
-        self.far().wait_send()
+        self.took(self.LAST, self.from_core.at[1])
+        self.sent(self.CORE, self.w)
+        self.sent(self.Z, self.w.at[0 : m.depth - 1, 0:2, 0, :, self.mine])
 
 
 class SmallSum:
@@ -636,10 +575,9 @@
         self.me, self.small, self.inbox = me, small, inbox
         self.sends, self.recvs, self.base = sends, recvs, base
 
-    def copy(self, k, dev):
+    def copy(self, k, src, dst, dev):
         return pltpu.make_async_remote_copy(
-            src_ref=self.small.at[k], dst_ref=self.inbox.at[k],
-            send_sem=self.sends.at[self.base + k], recv_sem=self.recvs.at[self.base + k],
+            src_ref=src, dst_ref=dst, send_sem=self.sends.at[self.base[0]], recv_sem=self.recvs.at[self.base[1] + k],
             device_id=dev, device_id_type=MESH_ID,
         )
 
@@ -647,30 +585,22 @@
         return (self.me.sib, self.me.xn, self.me.yn)[k]
 
     def step(self, k):
-        m = self.me
+        m, small, inbox = self.me, self.small, self.inbox
         if 1 <= k <= 3:
-            self.copy(k - 1, self.peer(k - 1)).wait()
-            self.small[k] = self.small[k - 1] + self.inbox[k - 1]
+            self.copy(k - 1, small.at[0], inbox.at[k - 1], m.sib).wait_recv()
+            small[k] = small[k - 1] + inbox[k - 1]
         if k <= 2:
-            self.copy(k, self.peer(k)).start()
+            self.copy(k, small.at[k], inbox.at[k], self.peer(k)).start()
         if k == 3:
             for o in range(1, m.depth):
-                self.z_copy(o).start()
+                self.copy(3, small.at[3], inbox.at[2 + o], m.at_z(m.ahead(o))).start()
         if k == 4:
-            total = self.small[3]
+            self.copy(3, inbox.at[3:], inbox.at[3:], m.sib).wait_recv()
+            total = small[3]
             for o in range(1, m.depth):
-                self.z_copy(o).wait()
-                total = total + self.inbox[2 + o]
-            self.small[4] = total
-
-    def z_copy(self, o):
-        m = self.me
-        at = self.base + 2 + o
-        return pltpu.make_async_remote_copy(
-            src_ref=self.small.at[3], dst_ref=self.inbox.at[2 + o],
-            send_sem=self.sends.at[at], recv_sem=self.recvs.at[at],
-            device_id=m.at_z(m.ahead(o)), device_id_type=MESH_ID,
-        )
+                total = total + inbox[2 + o]
+            small[4] = total
+            self.copy(3, inbox, inbox, m.sib).wait_send()
 
 
 def chunk_boxes(rows_a, width, rows_d, ff_c):
@@ -688,10 +618,10 @@
 
 
 def block_kernel(
-    depth, tokens, cot, idx, valid, wq, wk, wv, wo, up_in, down_in, gpad,
+    depth, tokens, cot, idx, valid, wq, wk, wv, wo, up_in, down_in, gain1, gain2, gain3,
     new_rows, new_grads, fa, fu, fd, small_out,
     wa, wu, wd, picked, up, cols, na, nmt, dd, qkv, probs, mixed, attn_out, act, dup, down, dnm,
-    gains, gbox, small, inbox,
+    gains, gpad, gbox, small, inbox,
     tok_sem, own_sem, out_sem, ag_send, ag_recv, rs_send, rs_recv, frees, opened, *boxes,
 ):
     seqs, slots = idx.shape
@@ -703,80 +633,69 @@
     me.greet()
     own = Owned(me, (wq, wk, wv, wo, up_in, down_in), wa, wu, wd, own_sem)
     ag = Gather(me, wa, wu, wd, ag_send, ag_recv)
-    gsem = 7 * Gather.SLOTS
+    sem_at = (20, 70)
     others = range(1, depth)
 
     def gain_copy(o):
         return pltpu.make_async_remote_copy(
-            src_ref=gpad, dst_ref=gbox.at[o - 1], send_sem=ag_send.at[gsem + o], recv_sem=ag_recv.at[gsem + o],
+            src_ref=gpad, dst_ref=gbox.at[o - 1], send_sem=rs_send.at[21], recv_sem=rs_recv.at[74],
             device_id=me.at_z(me.ahead(o)), device_id_type=MESH_ID,
         )
 
-    def spread(*arrays):
-        for a in arrays:
-            for o in others:
-                ag.spread(a, o)
-
-    def forward(*arrays):
-        for a in arrays:
-            for o in others:
-                ag.forward(a, o)
-
-    def across(*arrays):
-        for a in arrays:
-            ag.across(a)
-
     own.start(0)
+    own.start(1)
     picker = Picker(tokens, cot, picked, up, cols, (act, dup), tok_sem)
-    for a in range(1, 7):
+    picker.start(0)
+    for a in range(2, Gather.ARRAYS):
         own.start(a)
-    picker.start(0)
     own.wait(0)
     ag.send_z(0)
+    own.wait(1)
+    ag.send_z(1)
+    owned = gain1.shape[0]
+    spot = lax.broadcasted_iota(jnp.int32, (owned, width), 1) - lax.broadcasted_iota(jnp.int32, (owned, width), 0)
+    spot = jnp.where(spot == me.z * owned, 1.0, 0.0).astype(BF)
+    gpad[...] = jnp.zeros_like(gpad)
+    for i, g in enumerate((gain1, gain2, gain3)):
+        gpad[i : i + 1, :] = nn(g[...].astype(F32).reshape(1, owned).astype(BF), spot)
     for o in others:
         gain_copy(o).start()
-    for a in range(1, 7):
-        own.wait(a)
-        ag.send_z(a)
     picker.turn(idx, valid)
     picker.pick(0, slots, True)
+    for a in range(2, Gather.ARRAYS):
+        own.wait(a)
+    ag.slot(0)
     picker.pick(1, slots, True)
-    spread(0)
+    ag.slot(1)
     picker.pick(2, slots, True)
+    ag.slot(2)
     picker.pick(3, slots, False)
-    total = gpad[...].astype(F32)
+    ag.slot(3)
+    pltpu.make_async_remote_copy(
+        src_ref=gbox, dst_ref=gbox, send_sem=rs_send.at[21], recv_sem=rs_recv.at[74],
+        device_id=me.sib, device_id_type=MESH_ID,
+    ).wait()
+    total = gpad[...]
     for o in others:
-        gain_copy(o).wait()
-        total = total + gbox[o - 1].astype(F32)
-    gains[...] = total[:8]
+        total = total + gbox[o - 1]
+    gains[...] = total
     norm_phase(picked, gains, cols, na)
-    forward(0)
-    spread(1, 2)
-    across(0)
-    ag.ready(0)
-    qkv_phase(na, wa, qkv, scale)
-    spread(3, 4)
-    forward(1, 2)
+    ag.slot(4)
+    for m in range(3):
+        ag.ready(m)
+        qkv_one(na, wa, qkv, scale, m)
+        ag.slot(5 + m)
 
     @pl.loop(0, seqs)
     def _(s):
         attention_forward(idx, valid, cols, qkv, probs, mixed, s)
-
-        @pl.when(s == 0)
-        def _():
-            across(1, 2)
-            spread(5, 6)
-            forward(3, 4)
-
-        @pl.when(s == 1)
-        def _():
-            across(3, 4)
-            forward(5, 6)
-
-        @pl.when(s == 2)
-        def _():
-            across(5, 6)
-
+        for k in range(4):
+
+            @pl.when(s == k)
+            def _():
+                ag.slot(8 + k)
+
+    ag.ready(3)
     out_phase(mixed, wa, attn_out)
     mid_norm(picked, attn_out, up, gains, cols, na, nmt, dd)
 
@@ -804,9 +723,8 @@
     def result_copies(name):
         dst, i = finals[name]
         box = reducers[name].from_core
-        base = 2 * order.index(name)
         for h, core in ((0, me.core), (1, 1 - me.core)):
-            yield pltpu.make_async_copy(box.at[h], dst.at[i, :, :, :, half_of(dst, core)], out_sem.at[base + h])
+            yield pltpu.make_async_copy(box.at[h], dst.at[i, :, :, :, half_of(dst, core)], out_sem.at[{"u": 1, "d": 2}.get(name[0], 0)])
 
     def step(k, *names):
         for name in names:
@@ -816,47 +734,44 @@
                     c.start()
 
     for c in range(CHUNKS):
-        for a in (1 + 2 * c, 2 + 2 * c):
+        for a in (A_MATS + 2 * c, A_MATS + 1 + 2 * c):
             ag.ready(a)
 
         @pl.loop(0, 4)
         def _(n):
             mlp_up(na, dd, wu, wd, act, dup, c, n)
-
-        if c == 1:
-            step(2, "u0", "d0")
-        if c == 2:
-            step(4, "u0", "d0")
-            step(2, "u1", "d1")
+            if c > 0:
+
+                @pl.when(n == 1)
+                def _():
+                    step(2, "d%d" % (c - 1), "u%d" % (c - 1))
+
         mlp_down(act, wd, down, c)
         mlp_dnormed(dup, wu, dnm, c)
         if c == 2:
-            step(5, "u0", "d0")
-        ag.settle(1 + 2 * c)
-        ag.settle(2 + 2 * c)
+            step(4, "d0", "u0")
+        ag.settle(A_MATS + 2 * c)
+        ag.settle(A_MATS + 1 + 2 * c)
         mlp_grad_down(act, dd, wd, c)
         step(1, "d%d" % c)
         mlp_grad_up(nmt, dup, wu, c)
         step(1, "u%d" % c)
-        if c == 1:
-            step(3, "u0", "d0")
-        if c == 2:
-            step(3, "u1", "d1")
-            step(6, "u0", "d0")
+        if c > 0:
+            step(3, "d%d" % (c - 1), "u%d" % (c - 1))
     pl.semaphore_signal(opened, inc=1, device_id=me.sib, device_id_type=MESH_ID)
-    ag.settle(0)
+    for a in range(A_MATS):
+        ag.settle(a)
     datt, dmix = na, dd
     mid_backward(picked, attn_out, up, down, dnm, gains, cols, datt, dd, small.at[0])
     rows_out = pltpu.make_async_copy(dd, new_rows, tok_sem.at[0])
     rows_out.start()
-    step(2, "u2", "d2")
-    step(4, "u1", "d1")
-    step(7, "u0", "d0")
+    step(2, "d2", "u2")
     rows_out.wait()
     out_backward(datt, mixed, wa, dmix)
     pl.semaphore_wait(opened, 1)
     step(1, "o")
-    step(8, "u0", "d0")
+    step(4, "d1", "u1")
+    step(5, "d0", "u0")
     norm_again(picked, gains, cols, na)
 
     @pl.loop(0, seqs)
@@ -865,56 +780,66 @@
 
         @pl.when(s == 0)
         def _():
-            step(3, "u2", "d2")
-            step(5, "u1", "d1")
             step(2, "o")
+            step(6, "d0", "u0")
 
         @pl.when(s == 1)
         def _():
-            step(4, "u2", "d2")
-            step(6, "u1", "d1")
-            step(3, "o")
+            step(7, "d0", "u0")
 
         @pl.when(s == 2)
         def _():
-            step(5, "u2", "d2")
-            step(7, "u1", "d1")
-            step(4, "o")
+            step(3, "d2", "u2")
+            step(8, "d0", "u0")
+
+        @pl.when(s == 3)
+        def _():
+            step(3, "o")
 
     for m, name in enumerate("qkv"):
         terms[m][...] = grad_of(na, qkv[m]).reshape(wa.shape[1:])
         step(1, name)
+        if m == 0:
+            step(5, "d1", "u1")
         if m > 0:
             step(2, "qkv"[m - 1])
-    step(6, "u2", "d2")
-    step(8, "u1", "d1")
-    step(5, "o")
+    step(4, "d2", "u2", "o")
     qkv_normed(qkv, wa, down)
     step(2, "v")
+    step(3, "q")
+    step(6, "d1", "u1")
     first_backward(picked, up, down, dnm, gains, cols, dd, small.at[0])
     grads_out = pltpu.make_async_copy(dd, new_grads, tok_sem.at[1])
     grads_out.start()
-    sums = SmallSum(me, small, inbox, rs_send, rs_recv, 10 * Reduce.SLOTS)
+    sums = SmallSum(me, small, inbox, rs_send, rs_recv, sem_at)
     sums.step(0)
-    step(3, *"qkv")
-    step(7, "u2", "d2")
-    step(6, "o")
+    step(3, "k")
+    step(4, "q")
+    step(7, "d1", "u1")
     sums.step(1)
-    step(4, *"qkv")
+    step(5, "d2", "u2", "o")
+    step(3, "v")
+    step(4, "k")
     sums.step(2)
-    step(8, "u2", "d2")
-    step(7, "o")
+    step(6, "d2", "u2", "o")
+    step(4, "v")
+    step(8, "d1", "u1")
     sums.step(3)
-    step(5, *"qkv")
-    step(8, "o")
-    step(6, *"qkv")
+    step(5, "q")
+    step(7, "d2", "u2", "o")
+    step(5, "k")
+    step(6, "q")
     sums.step(4)
-    step(7, *"qkv")
+    step(5, "v")
+    step(6, "k")
+    step(7, "q")
+    step(8, "d2", "u2", "o")
+    step(6, "v")
+    step(7, "k", "v")
     step(8, *"qkv")
     small_out[...] = small[4]
-    for name in order:
-        for c in result_copies(name):
-            c.wait()
+    for i, dst in enumerate((fa, fu, fd)):
+        pltpu.make_async_copy(dst, dst, out_sem.at[i]).wait()
     grads_out.wait()
 
 
@@ -971,11 +896,10 @@
     sem = pltpu.SemaphoreType.DMA
     vmem = pltpu.VMEM
     z = lax.axis_index("fsdp")
-    gains3 = jnp.stack([gain_attn, gain_mlp, w_router])
-    gpad = lax.dynamic_update_slice(jnp.zeros((16, width), BF), gains3, (0, z * own))
+    gains3 = (gain_attn, gain_mlp, w_router)
     squares = [w.reshape(2, 2, rq, width) for w in (w_query, w_key, w_value, w_out)]
     sa, su, sdn = (A_MATS, depth, 2, 2, rq, width), (CHUNKS, depth, 2, 2, rq, cw), (CHUNKS, depth, 2, 2, dq, width)
-    nag, nrs = 7 * Gather.SLOTS + 8, 10 * Reduce.SLOTS + 8
+    narr = Gather.ARRAYS
     rows = (total, width)
     work = (4, 2, 2, total // 16, cw)
     regular = pltpu.SemaphoreType.REGULAR
@@ -986,20 +910,21 @@
             sd(rows, BF), sd(rows, BF), sd(sa[:1] + sa[2:], BF), sd(su[:1] + su[2:], BF), sd(sdn[:1] + sdn[2:], BF),
             sd((8, width), F32),
         ),
-        in_specs=[hbm, hbm, vm, vm] + [hbm] * 6 + [vm],
+        in_specs=[hbm, hbm, vm, vm] + [hbm] * 6 + [vm] * 3,
         out_specs=(hbm,) * 5 + (vm,),
         scratch_shapes=[
             vmem(sa, BF), vmem(su, BF), vmem(sdn, BF), vmem(rows, BF), vmem(rows, BF), vmem((total, 128), F32),
             vmem(rows, BF), vmem((width, total), BF), vmem(rows, BF), vmem((3,) + rows, BF), vmem((3,) + work, BF),
             vmem(rows, BF), vmem(rows, F32), vmem(work, BF), vmem(work, BF), vmem(rows, F32), vmem(rows, F32),
-            vmem((8, width), F32), vmem((depth - 1, 16, width), BF), vmem((5, 8, width), F32), vmem((2 + depth, 8, width), F32),
-            sem((2,)), sem((16,)), sem((20,)), sem((nag,)), sem((nag,)), sem((nrs,)), sem((nrs,)), regular((10,)), regular,
+            vmem((8, width), F32), vmem((8, width), F32), vmem((depth - 1, 8, width), F32), vmem((5, 8, width), F32), vmem((2 + depth, 8, width), F32),
+            sem((2,)), sem((2 * narr,)), sem((3,)), sem((2 * narr,)), sem((5 * narr,)),
+            sem((2 * narr + 2,)), sem((7 * narr + 5,)), regular((narr,)), regular,
         ]
         + chunk_boxes(rq, width, dq, cw),
         compiler_params=remote_params(0, 63),
     )(
         tokens.reshape(blocks), cotangent.reshape(blocks), row_index, row_valid, *squares,
-        w_up.reshape(2, 2, rq, ff), w_down.reshape(CHUNKS, 2, 2, dq, width), gpad,
+        w_up.reshape(2, 2, rq, ff), w_down.reshape(CHUNKS, 2, 2, dq, width), *gains3,
     )
     fa, fu, fd, sums = over_groups(groups, (fa, fu, fd, sums))
     out, grad, gq, gk, gv, go, gup, gdown = pl.pallas_call(
@@ -1011,7 +936,7 @@
         + [pl.BlockSpec((A_MATS, 1, rq, width), lambda s: (0, s, 0, 0)), pl.BlockSpec((CHUNKS, 1, rq, cw), lambda s: (0, s, 0, 0)), pl.BlockSpec((CHUNKS, 1, dq, width), lambda s: (0, s, 0, 0))],
         out_specs=[pl.BlockSpec((length, width), lambda s: (s, 0))] * 2 + [pl.BlockSpec((rq, width), lambda s: (s, 0))] * 4
         + [pl.BlockSpec((rq, ff), lambda s: (s, 0)), pl.BlockSpec((CHUNKS, 1, dq, width), lambda s: (0, s, 0, 0))],
-        compiler_params=pltpu.CompilerParams(vmem_limit_bytes=50 * 2**20),
+        compiler_params=pltpu.CompilerParams(vmem_limit_bytes=62 * 2**20),
     )(row_index, tokens, cotangent, new_rows, new_grads, fa.reshape(A_MATS, 4, rq, width), fu.reshape(CHUNKS, 4, rq, cw), fd.reshape(CHUNKS, 4, dq, width))
     vec = lax.dynamic_slice(sums, (0, z * own), (3, own))
     return (out, grad, gq, gk, gv, go, gup, gdown.reshape(w_down.shape), vec[0], vec[1], vec[2])

time: 231 us -> 199 us (0.86)
  Pallas kernels: 221 us -> 197 us
  local copies, waits for them, and re-layouts: 8.34 us -> 1.48 us
    pallas_call x1, Pallas kernels: 208 us -> 183 us  [body(): pl.pallas_call(functools.partial(block_kernel, depth), out_shape=(sd(rows...]
    unnamed x10 -> x0, local copies, waits for them, and re-layouts: 4.42 us -> none
where the time goes in v3:
time: 199 us
  Pallas kernels  197 us (99%)
    pallas_call x1, Pallas kernels, body(): pl.pallas_call(functools.partial(block_kernel, depth), out_shape=(sd(rows...  183 us
    pallas_call x1, Pallas kernels, body(): pl.pallas_call(place_kernel, grid=(seqs,), out_shape=(sd(tokens.shape, BF...  13.9 us

profile of v3, /device:TPU:0, one launch (start us, length us, event | category | flops | bytes accessed | tf_op | source)
XLA Modules:
  0.0 198.9 jit_solution(14666655518400056868)
XLA Ops:
  0.7 182.7 %shard_map.212 = (bf16[1024,768]{1,0:T(8,128)(2,1)}, bf16[1024,768]{1,0:T(8,128)(2,1)}, bf16[4,2,2,48,768]{4,3,2,1,0:T(8,128)(2,1)}, bf16[3,2,2,48,1024]{4,3,2,1...) custom-call(bf16[4,4,2,2,64,768]{5,4,3,2,1,0:T(8,128)(2,1)} %bitcast.15, ...), custom_call_target="tpu_custom_call" | custom-call | tf_op jit(solution)/shard_map/pallas_call | solution.py:907
  183.3 1.5 fusion
  184.8 13.9 %shard_map.213 = (bf16[4096,768]{1,0:T(8,128)(2,1)}, bf16[4096,768]{1,0:T(8,128)(2,1)}, f32[192,768]{1,0:T(8,128)}, f32[192,768]{1,0:T(8,128)}, f32[192,768]{1,0...) custom-call(s32[4,256]{1,0:T(4,128)} %idx.3, bf16[4096,768]{1,0:T(8,128)(2,1)} %tokens.1, ...), custom_call_target="tpu_custom_call" | custom-call | tf_op jit(solution)/shard_map/pallas_call | solution.py:930

commit v4 on v3

--- a/solution.py
+++ b/solution.py
@@ -188,12 +188,16 @@
 
 def mlp_up(nm, dd, wu, wd, act, dup, c, n):
     at = pl.ds(pl.multiple_of(n * 256, 256), 256)
-    u = nn(nm[...], flat(wu[c, :, :, :, :, at]))
-    dact = nt(dd[...], flat(wd[c, n]))
-    a, slope = gelu_both(u)
-    shape = act.shape[:4] + (256,)
-    act[:, :, :, :, at] = a.astype(BF).reshape(shape)
-    dup[:, :, :, :, at] = (slope * dact).astype(BF).reshape(shape)
+    w_up, w_down = flat(wu[c, :, :, :, :, at]), flat(wd[c, n])
+    tall = nm.shape[0] // act.shape[0]
+    for i in range(act.shape[0]):
+        rows = slice(i * tall, (i + 1) * tall)
+        u = nn(nm[rows, :], w_up)
+        dact = nt(dd[rows, :], w_down)
+        a, slope = gelu_both(u)
+        shape = act.shape[1:4] + (256,)
+        act[i, :, :, :, at] = a.astype(BF).reshape(shape)
+        dup[i, :, :, :, at] = (slope * dact).astype(BF).reshape(shape)
 
 
 def mlp_down(act, wd, down, c):
@@ -222,11 +226,11 @@
 
 
 def mlp_grad_up(nmt, dup, wu, c):
-    @pl.loop(0, dup.shape[-1] // 256)
+    @pl.loop(0, dup.shape[-1] // 512)
     def _(n):
-        at = pl.ds(pl.multiple_of(n * 256, 256), 256)
+        at = pl.ds(pl.multiple_of(n * 512, 512), 512)
         g = nn(nmt[...], flat(dup[:, :, :, :, at])).astype(BF)
-        wu[c, :, :, :, :, at] = g.reshape(wu.shape[1:5] + (256,))
+        wu[c, :, :, :, :, at] = g.reshape(wu.shape[1:5] + (512,))
 
 
 def mid_backward(picked, attn_out, up, down, dnm, gains, cols, datt, new_rows, small, tile=128):
@@ -275,7 +279,7 @@
     return jnp.concatenate(parts, axis=0)
 
 
-def qkv_normed(dqkv, wa, dnorm):
+def qkv_normed(dqkv, wa, dnorm, beat):
     total = dqkv.shape[1]
 
     @pl.loop(0, 4)
@@ -287,9 +291,10 @@
             + nt(dqkv[1, rows, :], flat(wa[1]))
             + nt(dqkv[2, rows, :], flat(wa[2]))
         )
-
-
-def first_backward(picked, up, dnorm, dhid, gains, cols, new_grads, small, tile=128):
+        beat(i)
+
+
+def first_backward(picked, up, dnorm, dhid, gains, cols, new_grads, small, beat, tile=128):
     total = picked.shape[0]
 
     @pl.loop(0, total // tile)
@@ -305,6 +310,7 @@
         d_first = r * (gains[0:1, :] * d - xr * mean)
         d_picked = d_first + dhid[rows, :] + cols[rows, DLOG : DLOG + 1] * gains[2:3, :]
         new_grads[rows, :] = (up[rows, :].astype(F32) + d_picked).astype(BF)
+        beat(i)
 
 
 MESH_ID = pl.DeviceIdType.MESH
@@ -421,16 +427,6 @@
         self.core_copy(a, m.core).wait_send()
         sent = ref.at[0 : m.depth - 1, :, :, :, half_of(ref, m.core)]
         self.copy(a, self.Z, sent, m.xn).wait_send()
-
-    def slot(self, t, ahead=2):
-        if t < self.ARRAYS:
-            self.spread(t)
-        if ahead <= t + ahead < self.ARRAYS:
-            self.send_z(t + ahead)
-        if 0 <= t - 1 < self.ARRAYS:
-            self.forward(t - 1)
-        if 0 <= t - 2 < self.ARRAYS:
-            self.across(t - 2)
 
 
 class Owned:
@@ -501,7 +497,7 @@
         return self.copy(kind, ref, ref, dev)
 
     def add(self, at, arrived):
-        self.w[at] = (self.w[at].astype(F32) + arrived.astype(F32)).astype(BF)
+        self.w[at] = self.w[at] + arrived
 
     def t1(self):
         self.copy(self.CORE, self.w.at[:, :, :, :, self.theirs], self.from_core, self.me.sib).start()
@@ -650,6 +646,7 @@
         own.start(a)
     own.wait(0)
     ag.send_z(0)
+    picker.turn(idx, valid)
     own.wait(1)
     ag.send_z(1)
     owned = gain1.shape[0]
@@ -660,17 +657,18 @@
         gpad[i : i + 1, :] = nn(g[...].astype(F32).reshape(1, owned).astype(BF), spot)
     for o in others:
         gain_copy(o).start()
-    picker.turn(idx, valid)
     picker.pick(0, slots, True)
     for a in range(2, Gather.ARRAYS):
         own.wait(a)
-    ag.slot(0)
+    ag.send_z(2)
+    ag.spread(0)
     picker.pick(1, slots, True)
-    ag.slot(1)
+    ag.send_z(3)
     picker.pick(2, slots, True)
-    ag.slot(2)
+    ag.send_z(4)
+    ag.forward(0)
+    ag.spread(1)
     picker.pick(3, slots, False)
-    ag.slot(3)
     pltpu.make_async_remote_copy(
         src_ref=gbox, dst_ref=gbox, send_sem=rs_send.at[21], recv_sem=rs_recv.at[74],
         device_id=me.sib, device_id_type=MESH_ID,
@@ -680,24 +678,55 @@
         total = total + gbox[o - 1]
     gains[...] = total
     norm_phase(picked, gains, cols, na)
-    ag.slot(4)
-    for m in range(3):
-        ag.ready(m)
-        qkv_one(na, wa, qkv, scale, m)
-        ag.slot(5 + m)
+    ag.across(0)
+    ag.send_z(5)
+    ag.forward(1)
+    ag.spread(2)
+    ag.ready(0)
+    qkv_one(na, wa, qkv, scale, 0)
+    ag.across(1)
+    ag.send_z(6)
+    ag.forward(2)
+    ag.ready(1)
+    qkv_one(na, wa, qkv, scale, 1)
+    ag.across(2)
+    ag.spread(3)
+    ag.ready(2)
+    qkv_one(na, wa, qkv, scale, 2)
+    ag.forward(3)
+    ag.spread(4)
+    ag.send_z(7)
 
     @pl.loop(0, seqs)
     def _(s):
         attention_forward(idx, valid, cols, qkv, probs, mixed, s)
-        for k in range(4):
-
-            @pl.when(s == k)
-            def _():
-                ag.slot(8 + k)
+
+        @pl.when(s == 0)
+        def _():
+            ag.across(3)
+            ag.spread(5)
+
+        @pl.when(s == 1)
+        def _():
+            ag.forward(4)
+            ag.send_z(8)
+            ag.send_z(9)
+
+        @pl.when(s == 2)
+        def _():
+            ag.forward(5)
+            ag.across(4)
+
+        @pl.when(s == 3)
+        def _():
+            ag.spread(6)
 
     ag.ready(3)
     out_phase(mixed, wa, attn_out)
+    ag.across(5)
     mid_norm(picked, attn_out, up, gains, cols, na, nmt, dd)
+    ag.forward(6)
+    ag.spread(7)
 
     ubox, dbox, abox = boxes[0:6], boxes[6:12], boxes[12:17]
     reducers = {}
@@ -746,15 +775,29 @@
                 def _():
                     step(2, "d%d" % (c - 1), "u%d" % (c - 1))
 
+        if c == 0:
+            ag.across(6)
+            ag.spread(8)
+            ag.forward(7)
+        if c == 1:
+            ag.across(9)
         mlp_down(act, wd, down, c)
         mlp_dnormed(dup, wu, dnm, c)
+        if c == 0:
+            ag.across(7)
+            ag.spread(9)
         if c == 2:
             step(4, "d0", "u0")
         ag.settle(A_MATS + 2 * c)
         ag.settle(A_MATS + 1 + 2 * c)
         mlp_grad_down(act, dd, wd, c)
         step(1, "d%d" % c)
+        if c == 0:
+            ag.forward(8)
         mlp_grad_up(nmt, dup, wu, c)
+        if c == 0:
+            ag.across(8)
+            ag.forward(9)
         step(1, "u%d" % c)
         if c > 0:
             step(3, "d%d" % (c - 1), "u%d" % (c - 1))
@@ -803,33 +846,44 @@
             step(5, "d1", "u1")
         if m > 0:
             step(2, "qkv"[m - 1])
-    step(4, "d2", "u2", "o")
-    qkv_normed(qkv, wa, down)
-    step(2, "v")
-    step(3, "q")
-    step(6, "d1", "u1")
-    first_backward(picked, up, down, dnm, gains, cols, dd, small.at[0])
+    step(4, "d2", "u2")
+
+    def at_beats(*todo):
+        def beat(i):
+            for k, work in todo:
+
+                @pl.when(i == k)
+                def _():
+                    for t, *names in work:
+                        step(t, *names)
+
+        return beat
+
+    qkv_normed(
+        qkv, wa, down, at_beats((0, [(2, "v")]), (1, [(4, "o")]), (2, [(3, "q")]), (3, [(6, "d1", "u1"), (3, "k")]))
+    )
+    first_backward(
+        picked, up, down, dnm, gains, cols, dd, small.at[0],
+        at_beats((2, [(7, "d1", "u1")]), (4, [(3, "v"), (4, "q")])),
+    )
     grads_out = pltpu.make_async_copy(dd, new_grads, tok_sem.at[1])
     grads_out.start()
     sums = SmallSum(me, small, inbox, rs_send, rs_recv, sem_at)
     sums.step(0)
-    step(3, "k")
-    step(4, "q")
-    step(7, "d1", "u1")
+    step(4, "k")
+    step(5, "d2", "u2")
     sums.step(1)
-    step(5, "d2", "u2", "o")
-    step(3, "v")
-    step(4, "k")
+    step(5, "o")
+    step(4, "v")
+    step(8, "d1", "u1")
     sums.step(2)
     step(6, "d2", "u2", "o")
-    step(4, "v")
-    step(8, "d1", "u1")
     sums.step(3)
     step(5, "q")
     step(7, "d2", "u2", "o")
     step(5, "k")
+    sums.step(4)
     step(6, "q")
-    sums.step(4)
     step(5, "v")
     step(6, "k")
     step(7, "q")
@@ -843,8 +897,8 @@
     grads_out.wait()
 
 
-def place_kernel(idx, tokens, cot, new_rows, new_grads, fa, fu, fd,
-                 out, grad, gq, gk, gv, go, gup, gdown):
+def place_kernel(depth, idx, tokens, cot, new_rows, new_grads, fa, fu, fd, sums,
+                 out, grad, gq, gk, gv, go, gup, gdown, g1, g2, g3):
     s = pl.program_id(0)
     length, slots = tokens.shape[0], idx.shape[1]
     spot = lax.broadcasted_iota(jnp.int32, (length, slots), 0)
@@ -853,6 +907,17 @@
     hot = hot.astype(BF)
     for src, rows, dst in ((tokens, new_rows, out), (cot, new_grads, grad)):
         dst[...] = jnp.where(hit, nn(hot, rows[...]), src[...].astype(F32)).astype(BF)
+    place_weights(fa, fu, fd, gq, gk, gv, go, gup, gdown)
+    own = g1.shape[0]
+    for k in range(depth):
+
+        @pl.when((s == 0) & (lax.axis_index("fsdp") == k))
+        def _():
+            for i, g in enumerate((g1, g2, g3)):
+                g[...] = sums[i, k * own : (k + 1) * own]
+
+
+def place_weights(fa, fu, fd, gq, gk, gv, go, gup, gdown):
     for m, g in enumerate((gq, gk, gv, go)):
         g[...] = fa[m, 0].astype(F32)
     quarter = 256
@@ -895,7 +960,6 @@
     hbm, vm = pl.BlockSpec(memory_space=pl.ANY), pl.BlockSpec(memory_space=pltpu.VMEM)
     sem = pltpu.SemaphoreType.DMA
     vmem = pltpu.VMEM
-    z = lax.axis_index("fsdp")
     gains3 = (gain_attn, gain_mlp, w_router)
     squares = [w.reshape(2, 2, rq, width) for w in (w_query, w_key, w_value, w_out)]
     sa, su, sdn = (A_MATS, depth, 2, 2, rq, width), (CHUNKS, depth, 2, 2, rq, cw), (CHUNKS, depth, 2, 2, dq, width)
@@ -927,19 +991,35 @@
         w_up.reshape(2, 2, rq, ff), w_down.reshape(CHUNKS, 2, 2, dq, width), *gains3,
     )
     fa, fu, fd, sums = over_groups(groups, (fa, fu, fd, sums))
-    out, grad, gq, gk, gv, go, gup, gdown = pl.pallas_call(
-        place_kernel,
+
+    def by_seq(*shape):
+        return pl.BlockSpec(shape, lambda i: (i,) + (0,) * (len(shape) - 1))
+
+    def by_quarter(*shape):
+        return pl.BlockSpec(shape, lambda i: (0, i) + (0,) * (len(shape) - 2))
+
+    out, grad, gq, gk, gv, go, gup, gdown, g1, g2, g3 = pl.pallas_call(
+        functools.partial(place_kernel, depth),
         grid=(seqs,),
-        out_shape=(sd(tokens.shape, BF), sd(tokens.shape, BF)) + (sd((own, width), F32),) * 4 + (sd((own, ff), F32), sd((CHUNKS, 4, dq, width), F32)),
-        in_specs=[pl.BlockSpec((seqs, slots), lambda s: (0, 0))] + [pl.BlockSpec((length, width), lambda s: (s, 0))] * 2
-        + [pl.BlockSpec((slots, width), lambda s: (s, 0))] * 2
-        + [pl.BlockSpec((A_MATS, 1, rq, width), lambda s: (0, s, 0, 0)), pl.BlockSpec((CHUNKS, 1, rq, cw), lambda s: (0, s, 0, 0)), pl.BlockSpec((CHUNKS, 1, dq, width), lambda s: (0, s, 0, 0))],
-        out_specs=[pl.BlockSpec((length, width), lambda s: (s, 0))] * 2 + [pl.BlockSpec((rq, width), lambda s: (s, 0))] * 4
-        + [pl.BlockSpec((rq, ff), lambda s: (s, 0)), pl.BlockSpec((CHUNKS, 1, dq, width), lambda s: (0, s, 0, 0))],
+        out_shape=(sd(tokens.shape, BF),) * 2
+        + (sd((own, width), F32),) * 4
+        + (sd((own, ff), F32), sd((CHUNKS, 4, dq, width), F32))
+        + (sd((own,), F32),) * 3,
+        in_specs=[pl.BlockSpec((seqs, slots), lambda i: (0, 0))]
+        + [by_seq(length, width)] * 2
+        + [by_seq(slots, width)] * 2
+        + [by_quarter(A_MATS, 1, rq, width), by_quarter(CHUNKS, 1, rq, cw), by_quarter(CHUNKS, 1, dq, width)]
+        + [pl.BlockSpec((8, width), lambda i: (0, 0))],
+        out_specs=[by_seq(length, width)] * 2
+        + [by_seq(rq, width)] * 4
+        + [by_seq(rq, ff), by_quarter(CHUNKS, 1, dq, width)]
+        + [pl.BlockSpec((own,), lambda i: (0,))] * 3,
         compiler_params=pltpu.CompilerParams(vmem_limit_bytes=62 * 2**20),
-    )(row_index, tokens, cotangent, new_rows, new_grads, fa.reshape(A_MATS, 4, rq, width), fu.reshape(CHUNKS, 4, rq, cw), fd.reshape(CHUNKS, 4, dq, width))
-    vec = lax.dynamic_slice(sums, (0, z * own), (3, own))
-    return (out, grad, gq, gk, gv, go, gup, gdown.reshape(w_down.shape), vec[0], vec[1], vec[2])
+    )(
+        row_index, tokens, cotangent, new_rows, new_grads, fa.reshape(A_MATS, 4, rq, width),
+        fu.reshape(CHUNKS, 4, rq, cw), fd.reshape(CHUNKS, 4, dq, width), sums,
+    )
+    return (out, grad, gq, gk, gv, go, gup, gdown.reshape(w_down.shape), g1, g2, g3)
 
 
 def solution(mesh):

time: 199 us -> 192 us (0.965)
  Pallas kernels: 197 us -> 191 us
    pallas_call x1, Pallas kernels: 183 us -> 177 us  [body(): pl.pallas_call(functools.partial(block_kernel, depth), out_shape=(sd(rows...]
where the time goes in v4:
time: 192 us
  Pallas kernels  191 us (99%)
    pallas_call x1, Pallas kernels, body(): pl.pallas_call(functools.partial(block_kernel, depth), out_shape=(sd(rows...  177 us
    pallas_call x1, Pallas kernels, body(): pl.pallas_call(functools.partial(place_kernel, depth), grid=(seqs,), out_...  14.2 us

profile of v4, /device:TPU:0, one launch (start us, length us, event | category | flops | bytes accessed | tf_op | source)
XLA Modules:
  0.0 191.6 jit_solution(12745813773097272065)
XLA Ops:
  0.6 176.5 %shard_map.212 = (bf16[1024,768]{1,0:T(8,128)(2,1)}, bf16[1024,768]{1,0:T(8,128)(2,1)}, bf16[4,2,2,48,768]{4,3,2,1,0:T(8,128)(2,1)}, bf16[3,2,2,48,1024]{4,3,2,1...) custom-call(bf16[4,4,2,2,64,768]{5,4,3,2,1,0:T(8,128)(2,1)} %bitcast.12, ...), custom_call_target="tpu_custom_call" | custom-call | tf_op jit(solution)/shard_map/pallas_call | solution.py:971
  177.2 14.2 %shard_map.213 = (bf16[4096,768]{1,0:T(8,128)(2,1)}, bf16[4096,768]{1,0:T(8,128)(2,1)}, f32[192,768]{1,0:T(8,128)}, f32[192,768]{1,0:T(8,128)}, f32[192,768]{1,0...) custom-call(s32[4,256]{1,0:T(4,128)} %idx.3, ...), custom_call_target="tpu_custom_call" | custom-call | tf_op jit(solution)/shard_map/pallas_call | solution.py:1001

commit v5 on v4

--- a/solution.py
+++ b/solution.py
@@ -871,26 +871,23 @@
     sums = SmallSum(me, small, inbox, rs_send, rs_recv, sem_at)
     sums.step(0)
     step(4, "k")
+    step(4, "v")
+    sums.step(1)
     step(5, "d2", "u2")
-    sums.step(1)
     step(5, "o")
-    step(4, "v")
-    step(8, "d1", "u1")
     sums.step(2)
+    step(5, "q")
+    step(5, "k")
+    sums.step(3)
+    step(5, "v")
     step(6, "d2", "u2", "o")
-    sums.step(3)
-    step(5, "q")
+    step(6, "q")
+    step(6, "k")
+    sums.step(4)
+    step(6, "v")
     step(7, "d2", "u2", "o")
-    step(5, "k")
-    sums.step(4)
-    step(6, "q")
-    step(5, "v")
-    step(6, "k")
-    step(7, "q")
-    step(8, "d2", "u2", "o")
-    step(6, "v")
-    step(7, "k", "v")
-    step(8, *"qkv")
+    step(7, "q", "k", "v")
+    step(8, "d1", "u1", "d2", "u2", "o", "q", "k", "v")
     small_out[...] = small[4]
     for i, dst in enumerate((fa, fu, fd)):
         pltpu.make_async_copy(dst, dst, out_sem.at[i]).wait()

time: 192 us -> 189 us (0.984)
  Pallas kernels: 191 us -> 188 us
    pallas_call x1, Pallas kernels: 177 us -> 174 us  [body(): pl.pallas_call(functools.partial(block_kernel, depth), out_shape=(sd(rows...]
where the time goes in v5:
time: 189 us
  Pallas kernels  188 us (99%)
    pallas_call x1, Pallas kernels, body(): pl.pallas_call(functools.partial(block_kernel, depth), out_shape=(sd(rows...  174 us
    pallas_call x1, Pallas kernels, body(): pl.pallas_call(functools.partial(place_kernel, depth), grid=(seqs,), out_...  14.2 us

profile of v5, /device:TPU:0, one launch (start us, length us, event | category | flops | bytes accessed | tf_op | source)
XLA Modules:
  0.0 188.9 jit_solution(3793594971370820850)
XLA Ops:
  0.6 173.9 %shard_map.212 = (bf16[1024,768]{1,0:T(8,128)(2,1)}, bf16[1024,768]{1,0:T(8,128)(2,1)}, bf16[4,2,2,48,768]{4,3,2,1,0:T(8,128)(2,1)}, bf16[3,2,2,48,1024]{4,3,2,1...) custom-call(bf16[4,4,2,2,64,768]{5,4,3,2,1,0:T(8,128)(2,1)} %bitcast.12, ...), custom_call_target="tpu_custom_call" | custom-call | tf_op jit(solution)/shard_map/pallas_call | solution.py:968
  174.5 14.2 %shard_map.213 = (bf16[4096,768]{1,0:T(8,128)(2,1)}, bf16[4096,768]{1,0:T(8,128)(2,1)}, f32[192,768]{1,0:T(8,128)}, f32[192,768]{1,0:T(8,128)}, f32[192,768]{1,0...) custom-call(s32[4,256]{1,0:T(4,128)} %idx.3, ...), custom_call_target="tpu_custom_call" | custom-call | tf_op jit(solution)/shard_map/pallas_call | solution.py:998

commit v6 on v5

--- a/solution.py
+++ b/solution.py
@@ -218,11 +218,11 @@
 
 
 def mlp_grad_down(act, dd, wd, c):
-    @pl.loop(0, act.shape[-1] // 256)
+    @pl.loop(0, act.shape[-1] // 512)
     def _(n):
-        at = pl.ds(pl.multiple_of(n * 256, 256), 256)
+        at = pl.ds(pl.multiple_of(n * 512, 512), 512)
         g = tn(flat(act[:, :, :, :, at]), dd[...]).astype(BF)
-        wd[c, n] = g.reshape(wd.shape[2:])
+        wd[c, pl.ds(2 * n, 2)] = g.reshape((2,) + wd.shape[2:])
 
 
 def mlp_grad_up(nmt, dup, wu, c):

time: 189 us -> 188 us (level)
  no operation moved by 1% of the time
where the time goes in v6:
time: 188 us
  Pallas kernels  187 us (99%)
    pallas_call x1, Pallas kernels, body(): pl.pallas_call(functools.partial(block_kernel, depth), out_shape=(sd(rows...  173 us
    pallas_call x1, Pallas kernels, body(): pl.pallas_call(functools.partial(place_kernel, depth), grid=(seqs,), out_...  14.2 us

profile of v6, /device:TPU:0, one launch (start us, length us, event | category | flops | bytes accessed | tf_op | source)
XLA Modules:
  0.0 188.2 jit_solution(2576874439570855981)
XLA Ops:
  0.6 173.2 %shard_map.212 = (bf16[1024,768]{1,0:T(8,128)(2,1)}, bf16[1024,768]{1,0:T(8,128)(2,1)}, bf16[4,2,2,48,768]{4,3,2,1,0:T(8,128)(2,1)}, bf16[3,2,2,48,1024]{4,3,2,1...) custom-call(bf16[4,4,2,2,64,768]{5,4,3,2,1,0:T(8,128)(2,1)} %bitcast.12, ...), custom_call_target="tpu_custom_call" | custom-call | tf_op jit(solution)/shard_map/pallas_call | solution.py:968
  173.8 14.2 %shard_map.213 = (bf16[4096,768]{1,0:T(8,128)(2,1)}, bf16[4096,768]{1,0:T(8,128)(2,1)}, f32[192,768]{1,0:T(8,128)}, f32[192,768]{1,0:T(8,128)}, f32[192,768]{1,0...) custom-call(s32[4,256]{1,0:T(4,128)} %idx.3, ...), custom_call_target="tpu_custom_call" | custom-call | tf_op jit(solution)/shard_map/pallas_call | solution.py:998
